TPU v7x, 768 devices: a whole 4x8x12 slice. The times are simulated.
768 devices in a mesh: dom: 192 (over y, z, core), sub: 4 (over x).
Axes of the slice: x: 4, y: 8, z: 12, core: 2. Of those that a mesh axis runs over, the one named last changes fastest.
Arguments:
- start_vector: float32 [192, 4, 16, 128], P('dom', 'sub')
- blocks: bfloat16 [192, 4, 16, 7, 128, 128], P('dom', 'sub')
- columns: int32 [192, 4, 16, 7], P('dom', 'sub'), may hold values from 0 to 143, as said below
- shifts: float32 [8], replicated, may hold values from 1.2 to 1.8
Outputs:
- basis: float32 [9, 192, 4, 16, 128], P(None, 'dom', 'sub')
- factor: float32 [9, 9], replicated
Inputs may be any that keep to these rules, and one draw needn't show every extreme that they name: `columns`: entry 0 of block row r is the block row itself, slot 64 + r; other entries name any slot of the neighbourhood, repeats allowed.
All inputs are finite; a program needn't handle non-finite values.
Results may differ from a plain program's by a relative error of at most 0.0059.
Values may be sent and summed in bfloat16 or wider, within the bound.
No kernel may reach another device: no remote copies, remote signals or barrier semaphores. Data moves between devices by JAX's collectives and lax.ppermute only.
A program may use at most 32 MiB of HBM per device.

v0:
```python
import jax
import jax.numpy as jnp
from jax import lax
from jax.sharding import PartitionSpec as P

S = 8
S1 = 9


def extended(value, sides, width):
    for axis, dim in sides:
        peers, length = (lax.axis_size(axis), value.shape[dim])
        up = [(i, (i + 1) % peers) for i in range(peers - 1)]
        down = [(j, i) for i, j in up]
        last = lax.slice_in_dim(value, length - width, length, axis=dim)
        initial = lax.slice_in_dim(value, 0, width, axis=dim)
        before = lax.ppermute(last, axis, up)
        after = lax.ppermute(initial, axis, down)
        value = jnp.concatenate([before, value, after], axis=dim)
    return value


def neighbourhood(rounded):
    padded = extended(rounded, (("dom", 0), ("sub", 1)), 1)
    return padded.reshape(-1, rounded.shape[3])


def apply_matrix(field, local_blocks, local_columns):
    rounded = field.astype(jnp.bfloat16)
    pool = neighbourhood(rounded)
    picked = pool[local_columns]
    image = jnp.einsum("rnij,rnj->ri", local_blocks, picked, preferred_element_type=jnp.float32)
    return image.reshape(field.shape)


def on_device(start_vector, blocks, columns, shifts):
    local_blocks = blocks[0, 0]
    local_columns = columns[0, 0]
    vectors = [start_vector]
    for section in range(S):
        image = apply_matrix(vectors[-1], local_blocks, local_columns)
        vectors.append(image - shifts[section] * vectors[-1])
    basis = jnp.stack(vectors, axis=0)
    flat = basis.reshape(S1, -1)
    partial_gram = jnp.dot(flat, flat.T, precision=lax.Precision.HIGHEST)
    total_rows = lax.axis_size("dom") * lax.axis_size("sub") * flat.shape[1]
    gram = lax.psum(partial_gram, ("dom", "sub")) / total_rows
    factor = jnp.linalg.cholesky(gram).T
    return (basis, factor)


def solution(mesh):
    return jax.shard_map(
        on_device,
        mesh=mesh,
        in_specs=(
            P("dom", "sub", None, None),
            P("dom", "sub", None, None, None, None),
            P("dom", "sub", None, None),
            P(),
        ),
        out_specs=(P(None, "dom", "sub", None, None), P()),
        check_vma=False,
    )
```

profile of v0, /device:TPU:33, one launch (start us, length us, event | category | flops | bytes accessed | tf_op | source)
XLA Modules:
  0.0 302.9 jit_solution(13560555821499858625)
XLA Ops:
  1.4 2.6 collective-permute-start.1
  4.0 3.9 %collective-permute-start = (bf16[1,1,16,128]{3,2,1,0:T(8,128)(2,1)S(1)}, bf16[1,1,16,128]{3,2,1,0:T(8,128)(2,1)S(1)}, u32[]{:S(2)}, u32[]{:S(2)}) collective-permute-start(bf16[1,1,16,128]{3,2,1,0:T(8,128)(2,1)S(1)} %convert_element_type.24), channel_id=1, source_target_pairs={{0,4},{4,8},{8,12},{12,16},{16,20},{20,24},{24,28},{28,32},{32,36}... | collective-permute-start | bytes 12296 | tf_op jit(solution)/shard_map/ppermute | solution.py:17
  10.4 8.2 %collective-permute-done = bf16[1,1,16,128]{3,2,1,0:T(8,128)(2,1)S(1)} collective-permute-done((bf16[1,1,16,128]{3,2,1,0:T(8,128)(2,1)S(1)}, bf16[1,1,16,128]{3,2,1,0:T(8,128)(2,1)S(1)}, u32[]{:S(2)}, u32[]{:S(2)}) %collective-permute-start) | collective-permute-done | bytes 4128 | tf_op jit(solution)/shard_map/ppermute | solution.py:17
  19.8 4.0 %collective-permute-start.2 = (bf16[3,1,16,128]{3,2,1,0:T(8,128)(2,1)S(1)}, bf16[3,1,16,128]{3,2,1,0:T(8,128)(2,1)S(1)}, u32[]{:S(2)}, u32[]{:S(2)}) collective-permute-start(bf16[3,1,16,128]{3,2,1,0:T(8,128)(2,1)S(1)} %pad_maximum_fusion.8), channel_id=1, source_target_pairs={{0,1},{1,2},{2,3},{4,5},{5,6},{6,7},{8,9},{9,10},{10,11},{12,13},{... | collective-permute-start | bytes 36872 | tf_op jit(solution)/shard_map/ppermute | solution.py:17
  25.4 3.2 %fusion.14 = f32[16,1,128,1]{2,1,3,0:T(1,128)S(1)} fusion(bf16[16,7,128,1]{2,3,1,0:T(2,128)(2,1)S(1)} %reshape.198, bf16[1,1,16,7,128,128]{5,4,3,2,1,0:T(8,128)(2,1)} %param.5), kind=kOutput, calls=%fused_computation.22 | convolution fusion | flops 3670016 | bytes 3706880 | tf_op jit(solution)/shard_map/rnij,rnj->ri/dot_general | solution.py:32
  29.3 8.7 %collective-permute-start.5 = (bf16[1,1,16,128]{3,2,1,0:T(8,128)(2,1)S(1)}, bf16[1,1,16,128]{3,2,1,0:T(8,128)(2,1)S(1)}, u32[]{:S(2)}, u32[]{:S(2)}) collective-permute-start(bf16[1,1,16,128]{3,2,1,0:T(8,128)(2,1)S(1)} %get-tuple-element.18), channel_id=1, source_target_pairs={{4,0},{8,4},{12,8},{16,12},{20,16},{24,20},{28,24},{32,28},{36,32}... | collective-permute-start | bytes 12296 | tf_op jit(solution)/shard_map/ppermute | solution.py:18
  38.0 1.9 collective-permute-start.4
  42.4 4.5 %collective-permute-start.6 = (bf16[3,1,16,128]{3,2,1,0:T(8,128)(2,1)S(1)}, bf16[3,1,16,128]{3,2,1,0:T(8,128)(2,1)S(1)}, u32[]{:S(2)}, u32[]{:S(2)}) collective-permute-start(bf16[3,1,16,128]{3,2,1,0:T(8,128)(2,1)S(1)} %pad_maximum_fusion.9), channel_id=1, source_target_pairs={{0,1},{1,2},{2,3},{4,5},{5,6},{6,7},{8,9},{9,10},{10,11},{12,13},{... | collective-permute-start | bytes 36872 | tf_op jit(solution)/shard_map/ppermute | solution.py:17
  48.5 3.2 %fusion.12 = f32[16,1,128,1]{2,1,3,0:T(1,128)S(1)} fusion(bf16[16,7,128,1]{2,3,1,0:T(2,128)(2,1)S(1)} %reshape.200, bf16[1,1,16,7,128,128]{5,4,3,2,1,0:T(8,128)(2,1)} %param.5), kind=kOutput, calls=%fused_computation.20 | convolution fusion | flops 3670016 | bytes 3706880 | tf_op jit(solution)/shard_map/rnij,rnj->ri/dot_general | solution.py:32
  52.3 8.0 %collective-permute-start.9 = (bf16[1,1,16,128]{3,2,1,0:T(8,128)(2,1)S(1)}, bf16[1,1,16,128]{3,2,1,0:T(8,128)(2,1)S(1)}, u32[]{:S(2)}, u32[]{:S(2)}) collective-permute-start(bf16[1,1,16,128]{3,2,1,0:T(8,128)(2,1)S(1)} %get-tuple-element.16), channel_id=1, source_target_pairs={{4,0},{8,4},{12,8},{16,12},{20,16},{24,20},{28,24},{32,28},{36,32}... | collective-permute-start | bytes 12296 | tf_op jit(solution)/shard_map/ppermute | solution.py:18
  60.3 1.9 collective-permute-start.8
  64.6 4.5 %collective-permute-start.10 = (bf16[3,1,16,128]{3,2,1,0:T(8,128)(2,1)S(1)}, bf16[3,1,16,128]{3,2,1,0:T(8,128)(2,1)S(1)}, u32[]{:S(2)}, u32[]{:S(2)}) collective-permute-start(bf16[3,1,16,128]{3,2,1,0:T(8,128)(2,1)S(1)} %pad_maximum_fusion.10), channel_id=1, source_target_pairs={{0,1},{1,2},{2,3},{4,5},{5,6},{6,7},{8,9},{9,10},{10,11},{12,13},{... | collective-permute-start | bytes 36872 | tf_op jit(solution)/shard_map/ppermute | solution.py:17
  70.7 3.2 %fusion.10 = f32[16,1,128,1]{2,1,3,0:T(1,128)S(1)} fusion(bf16[16,7,128,1]{2,3,1,0:T(2,128)(2,1)S(1)} %reshape.202, bf16[1,1,16,7,128,128]{5,4,3,2,1,0:T(8,128)(2,1)} %param.5), kind=kOutput, calls=%fused_computation.18 | convolution fusion | flops 3670016 | bytes 3706880 | tf_op jit(solution)/shard_map/rnij,rnj->ri/dot_general | solution.py:32
  74.6 8.0 %collective-permute-start.13 = (bf16[1,1,16,128]{3,2,1,0:T(8,128)(2,1)S(1)}, bf16[1,1,16,128]{3,2,1,0:T(8,128)(2,1)S(1)}, u32[]{:S(2)}, u32[]{:S(2)}) collective-permute-start(bf16[1,1,16,128]{3,2,1,0:T(8,128)(2,1)S(1)} %get-tuple-element.14), channel_id=1, source_target_pairs={{4,0},{8,4},{12,8},{16,12},{20,16},{24,20},{28,24},{32,28},{36,32}... | collective-permute-start | bytes 12296 | tf_op jit(solution)/shard_map/ppermute | solution.py:18
  82.5 1.9 collective-permute-start.12
  86.9 4.5 %collective-permute-start.14 = (bf16[3,1,16,128]{3,2,1,0:T(8,128)(2,1)S(1)}, bf16[3,1,16,128]{3,2,1,0:T(8,128)(2,1)S(1)}, u32[]{:S(2)}, u32[]{:S(2)}) collective-permute-start(bf16[3,1,16,128]{3,2,1,0:T(8,128)(2,1)S(1)} %pad_maximum_fusion.11), channel_id=1, source_target_pairs={{0,1},{1,2},{2,3},{4,5},{5,6},{6,7},{8,9},{9,10},{10,11},{12,13},{... | collective-permute-start | bytes 36872 | tf_op jit(solution)/shard_map/ppermute | solution.py:17
  93.0 3.2 %fusion.8 = f32[16,1,128,1]{2,1,3,0:T(1,128)S(1)} fusion(bf16[16,7,128,1]{2,3,1,0:T(2,128)(2,1)S(1)} %reshape.204, bf16[1,1,16,7,128,128]{5,4,3,2,1,0:T(8,128)(2,1)} %param.5), kind=kOutput, calls=%fused_computation.16 | convolution fusion | flops 3670016 | bytes 3706880 | tf_op jit(solution)/shard_map/rnij,rnj->ri/dot_general | solution.py:32
  96.9 8.0 %collective-permute-start.17 = (bf16[1,1,16,128]{3,2,1,0:T(8,128)(2,1)S(1)}, bf16[1,1,16,128]{3,2,1,0:T(8,128)(2,1)S(1)}, u32[]{:S(2)}, u32[]{:S(2)}) collective-permute-start(bf16[1,1,16,128]{3,2,1,0:T(8,128)(2,1)S(1)} %get-tuple-element.12), channel_id=1, source_target_pairs={{4,0},{8,4},{12,8},{16,12},{20,16},{24,20},{28,24},{32,28},{36,32}... | collective-permute-start | bytes 12296 | tf_op jit(solution)/shard_map/ppermute | solution.py:18
  104.8 1.9 collective-permute-start.16
  109.2 4.5 %collective-permute-start.18 = (bf16[3,1,16,128]{3,2,1,0:T(8,128)(2,1)S(1)}, bf16[3,1,16,128]{3,2,1,0:T(8,128)(2,1)S(1)}, u32[]{:S(2)}, u32[]{:S(2)}) collective-permute-start(bf16[3,1,16,128]{3,2,1,0:T(8,128)(2,1)S(1)} %pad_maximum_fusion.12), channel_id=1, source_target_pairs={{0,1},{1,2},{2,3},{4,5},{5,6},{6,7},{8,9},{9,10},{10,11},{12,13},{... | collective-permute-start | bytes 36872 | tf_op jit(solution)/shard_map/ppermute | solution.py:17
  115.3 3.2 %fusion.6 = f32[16,1,128,1]{2,1,3,0:T(1,128)S(1)} fusion(bf16[16,7,128,1]{2,3,1,0:T(2,128)(2,1)S(1)} %reshape.206, bf16[1,1,16,7,128,128]{5,4,3,2,1,0:T(8,128)(2,1)} %param.5), kind=kOutput, calls=%fused_computation.14 | convolution fusion | flops 3670016 | bytes 3706880 | tf_op jit(solution)/shard_map/rnij,rnj->ri/dot_general | solution.py:32
  119.1 8.0 %collective-permute-start.21 = (bf16[1,1,16,128]{3,2,1,0:T(8,128)(2,1)S(1)}, bf16[1,1,16,128]{3,2,1,0:T(8,128)(2,1)S(1)}, u32[]{:S(2)}, u32[]{:S(2)}) collective-permute-start(bf16[1,1,16,128]{3,2,1,0:T(8,128)(2,1)S(1)} %get-tuple-element.10), channel_id=1, source_target_pairs={{4,0},{8,4},{12,8},{16,12},{20,16},{24,20},{28,24},{32,28},{36,32}... | collective-permute-start | bytes 12296 | tf_op jit(solution)/shard_map/ppermute | solution.py:18
  127.1 1.9 collective-permute-start.20
  131.4 4.5 %collective-permute-start.22 = (bf16[3,1,16,128]{3,2,1,0:T(8,128)(2,1)S(1)}, bf16[3,1,16,128]{3,2,1,0:T(8,128)(2,1)S(1)}, u32[]{:S(2)}, u32[]{:S(2)}) collective-permute-start(bf16[3,1,16,128]{3,2,1,0:T(8,128)(2,1)S(1)} %pad_maximum_fusion.13), channel_id=1, source_target_pairs={{0,1},{1,2},{2,3},{4,5},{5,6},{6,7},{8,9},{9,10},{10,11},{12,13},{... | collective-permute-start | bytes 36872 | tf_op jit(solution)/shard_map/ppermute | solution.py:17
  137.5 3.2 %fusion.4 = f32[16,1,128,1]{2,1,3,0:T(1,128)S(1)} fusion(bf16[16,7,128,1]{2,3,1,0:T(2,128)(2,1)S(1)} %reshape.208, bf16[1,1,16,7,128,128]{5,4,3,2,1,0:T(8,128)(2,1)} %param.5), kind=kOutput, calls=%fused_computation.12 | convolution fusion | flops 3670016 | bytes 3706880 | tf_op jit(solution)/shard_map/rnij,rnj->ri/dot_general | solution.py:32
  141.4 8.0 %collective-permute-start.25 = (bf16[1,1,16,128]{3,2,1,0:T(8,128)(2,1)S(1)}, bf16[1,1,16,128]{3,2,1,0:T(8,128)(2,1)S(1)}, u32[]{:S(2)}, u32[]{:S(2)}) collective-permute-start(bf16[1,1,16,128]{3,2,1,0:T(8,128)(2,1)S(1)} %get-tuple-element.8), channel_id=1, source_target_pairs={{4,0},{8,4},{12,8},{16,12},{20,16},{24,20},{28,24},{32,28},{36,32}... | collective-permute-start | bytes 12296 | tf_op jit(solution)/shard_map/ppermute | solution.py:18
  153.7 4.5 %collective-permute-start.26 = (bf16[3,1,16,128]{3,2,1,0:T(8,128)(2,1)S(1)}, bf16[3,1,16,128]{3,2,1,0:T(8,128)(2,1)S(1)}, u32[]{:S(2)}, u32[]{:S(2)}) collective-permute-start(bf16[3,1,16,128]{3,2,1,0:T(8,128)(2,1)S(1)} %pad_maximum_fusion.14), channel_id=1, source_target_pairs={{0,1},{1,2},{2,3},{4,5},{5,6},{6,7},{8,9},{9,10},{10,11},{12,13},{... | collective-permute-start | bytes 36872 | tf_op jit(solution)/shard_map/ppermute | solution.py:17
  159.8 3.2 %fusion.2 = f32[16,1,128,1]{2,1,3,0:T(1,128)S(1)} fusion(bf16[16,7,128,1]{2,3,1,0:T(2,128)(2,1)S(1)} %reshape.210, bf16[1,1,16,7,128,128]{5,4,3,2,1,0:T(8,128)(2,1)} %param.5), kind=kOutput, calls=%fused_computation.10 | convolution fusion | flops 3670016 | bytes 3706880 | tf_op jit(solution)/shard_map/rnij,rnj->ri/dot_general | solution.py:32
  163.8 8.0 %collective-permute-start.29 = (bf16[1,1,16,128]{3,2,1,0:T(8,128)(2,1)S(1)}, bf16[1,1,16,128]{3,2,1,0:T(8,128)(2,1)S(1)}, u32[]{:S(2)}, u32[]{:S(2)}) collective-permute-start(bf16[1,1,16,128]{3,2,1,0:T(8,128)(2,1)S(1)} %get-tuple-element.6), channel_id=1, source_target_pairs={{4,0},{8,4},{12,8},{16,12},{20,16},{24,20},{28,24},{32,28},{36,32}... | collective-permute-start | bytes 12296 | tf_op jit(solution)/shard_map/ppermute | solution.py:18
  176.1 4.5 %collective-permute-start.30 = (bf16[3,1,16,128]{3,2,1,0:T(8,128)(2,1)S(1)}, bf16[3,1,16,128]{3,2,1,0:T(8,128)(2,1)S(1)}, u32[]{:S(2)}, u32[]{:S(2)}) collective-permute-start(bf16[3,1,16,128]{3,2,1,0:T(8,128)(2,1)S(1)} %pad_maximum_fusion.15), channel_id=1, source_target_pairs={{0,1},{1,2},{2,3},{4,5},{5,6},{6,7},{8,9},{9,10},{10,11},{12,13},{... | collective-permute-start | bytes 36872 | tf_op jit(solution)/shard_map/ppermute | solution.py:17
  182.2 3.2 %fusion = f32[16,1,128,1]{2,1,3,0:T(1,128)S(1)} fusion(bf16[16,7,128,1]{2,3,1,0:T(2,128)(2,1)S(1)} %reshape.212, bf16[1,1,16,7,128,128]{5,4,3,2,1,0:T(8,128)(2,1)} %param.5), kind=kOutput, calls=%fused_computation.8 | convolution fusion | flops 3670016 | bytes 3706880 | tf_op jit(solution)/shard_map/rnij,rnj->ri/dot_general | solution.py:32
  187.2 112.8 %psum.7 = f32[9,9]{0,1:T(8,128)S(1)} all-reduce(f32[9,9]{0,1:T(8,128)S(1)} %convolution_bitcast_fusion), channel_id=1, replica_groups=mesh['dom'=192,'sub'=4] {'dom','sub'}, use_global_device_ids=true, to_apply=%region_0.0 | all-reduce | flops 81 | bytes 648 | tf_op jit(solution)/shard_map/psum | solution.py:47
  (100 shorter events, 46.7 us)
Async XLA Ops:
  1.4 9.0 %collective-permute-start.1 = (bf16[1,1,16,128]{3,2,1,0:T(8,128)(2,1)S(1)}, bf16[1,1,16,128]{3,2,1,0:T(8,128)(2,1)S(1)}, u32[]{:S(2)}, u32[]{:S(2)}) collective-permute-start(bf16[1,1,16,128]{3,2,1,0:T(8,128)(2,1)S(1)} %convert_element_type.24), channel_id=1, source_target_pairs={{4,0},{8,4},{12,8},{16,12},{20,16},{24,20},{28,24},{32,28},{36,32}... | collective-permute-start | bytes 12296 | tf_op jit(solution)/shard_map/ppermute | solution.py:18
  4.0 14.6 %collective-permute-start = (bf16[1,1,16,128]{3,2,1,0:T(8,128)(2,1)S(1)}, bf16[1,1,16,128]{3,2,1,0:T(8,128)(2,1)S(1)}, u32[]{:S(2)}, u32[]{:S(2)}) collective-permute-start(bf16[1,1,16,128]{3,2,1,0:T(8,128)(2,1)S(1)} %convert_element_type.24), channel_id=1, source_target_pairs={{0,4},{4,8},{8,12},{12,16},{16,20},{20,24},{24,28},{28,32},{32,36}... | collective-permute-start | bytes 12296 | tf_op jit(solution)/shard_map/ppermute | solution.py:17
  18.6 5.3 %collective-permute-start.3 = (bf16[3,1,16,128]{3,2,1,0:T(8,128)(2,1)S(1)}, bf16[3,1,16,128]{3,2,1,0:T(8,128)(2,1)S(1)}, u32[]{:S(2)}, u32[]{:S(2)}) collective-permute-start(bf16[3,1,16,128]{3,2,1,0:T(8,128)(2,1)S(1)} %pad_maximum_fusion.8), channel_id=1, source_target_pairs={{1,0},{2,1},{3,2},{5,4},{6,5},{7,6},{9,8},{10,9},{11,10},{13,12},{... | collective-permute-start | bytes 36872 | tf_op jit(solution)/shard_map/ppermute | solution.py:18
  19.8 4.8 %collective-permute-start.2 = (bf16[3,1,16,128]{3,2,1,0:T(8,128)(2,1)S(1)}, bf16[3,1,16,128]{3,2,1,0:T(8,128)(2,1)S(1)}, u32[]{:S(2)}, u32[]{:S(2)}) collective-permute-start(bf16[3,1,16,128]{3,2,1,0:T(8,128)(2,1)S(1)} %pad_maximum_fusion.8), channel_id=1, source_target_pairs={{0,1},{1,2},{2,3},{4,5},{5,6},{6,7},{8,9},{9,10},{10,11},{12,13},{... | collective-permute-start | bytes 36872 | tf_op jit(solution)/shard_map/ppermute | solution.py:17
  29.3 10.7 %collective-permute-start.5 = (bf16[1,1,16,128]{3,2,1,0:T(8,128)(2,1)S(1)}, bf16[1,1,16,128]{3,2,1,0:T(8,128)(2,1)S(1)}, u32[]{:S(2)}, u32[]{:S(2)}) collective-permute-start(bf16[1,1,16,128]{3,2,1,0:T(8,128)(2,1)S(1)} %get-tuple-element.18), channel_id=1, source_target_pairs={{4,0},{8,4},{12,8},{16,12},{20,16},{24,20},{28,24},{32,28},{36,32}... | collective-permute-start | bytes 12296 | tf_op jit(solution)/shard_map/ppermute | solution.py:18
  38.0 3.1 %collective-permute-start.4 = (bf16[1,1,16,128]{3,2,1,0:T(8,128)(2,1)S(1)}, bf16[1,1,16,128]{3,2,1,0:T(8,128)(2,1)S(1)}, u32[]{:S(2)}, u32[]{:S(2)}) collective-permute-start(bf16[1,1,16,128]{3,2,1,0:T(8,128)(2,1)S(1)} %get-tuple-element.18), channel_id=1, source_target_pairs={{0,4},{4,8},{8,12},{12,16},{16,20},{20,24},{24,28},{28,32},{32,36}... | collective-permute-start | bytes 12296 | tf_op jit(solution)/shard_map/ppermute | solution.py:17
  41.1 5.8 %collective-permute-start.7 = (bf16[3,1,16,128]{3,2,1,0:T(8,128)(2,1)S(1)}, bf16[3,1,16,128]{3,2,1,0:T(8,128)(2,1)S(1)}, u32[]{:S(2)}, u32[]{:S(2)}) collective-permute-start(bf16[3,1,16,128]{3,2,1,0:T(8,128)(2,1)S(1)} %pad_maximum_fusion.9), channel_id=1, source_target_pairs={{1,0},{2,1},{3,2},{5,4},{6,5},{7,6},{9,8},{10,9},{11,10},{13,12},{... | collective-permute-start | bytes 36872 | tf_op jit(solution)/shard_map/ppermute | solution.py:18
  42.4 5.4 %collective-permute-start.6 = (bf16[3,1,16,128]{3,2,1,0:T(8,128)(2,1)S(1)}, bf16[3,1,16,128]{3,2,1,0:T(8,128)(2,1)S(1)}, u32[]{:S(2)}, u32[]{:S(2)}) collective-permute-start(bf16[3,1,16,128]{3,2,1,0:T(8,128)(2,1)S(1)} %pad_maximum_fusion.9), channel_id=1, source_target_pairs={{0,1},{1,2},{2,3},{4,5},{5,6},{6,7},{8,9},{9,10},{10,11},{12,13},{... | collective-permute-start | bytes 36872 | tf_op jit(solution)/shard_map/ppermute | solution.py:17
  52.3 9.9 %collective-permute-start.9 = (bf16[1,1,16,128]{3,2,1,0:T(8,128)(2,1)S(1)}, bf16[1,1,16,128]{3,2,1,0:T(8,128)(2,1)S(1)}, u32[]{:S(2)}, u32[]{:S(2)}) collective-permute-start(bf16[1,1,16,128]{3,2,1,0:T(8,128)(2,1)S(1)} %get-tuple-element.16), channel_id=1, source_target_pairs={{4,0},{8,4},{12,8},{16,12},{20,16},{24,20},{28,24},{32,28},{36,32}... | collective-permute-start | bytes 12296 | tf_op jit(solution)/shard_map/ppermute | solution.py:18
  60.3 3.1 %collective-permute-start.8 = (bf16[1,1,16,128]{3,2,1,0:T(8,128)(2,1)S(1)}, bf16[1,1,16,128]{3,2,1,0:T(8,128)(2,1)S(1)}, u32[]{:S(2)}, u32[]{:S(2)}) collective-permute-start(bf16[1,1,16,128]{3,2,1,0:T(8,128)(2,1)S(1)} %get-tuple-element.16), channel_id=1, source_target_pairs={{0,4},{4,8},{8,12},{12,16},{16,20},{20,24},{24,28},{28,32},{32,36}... | collective-permute-start | bytes 12296 | tf_op jit(solution)/shard_map/ppermute | solution.py:17
  63.3 5.8 %collective-permute-start.11 = (bf16[3,1,16,128]{3,2,1,0:T(8,128)(2,1)S(1)}, bf16[3,1,16,128]{3,2,1,0:T(8,128)(2,1)S(1)}, u32[]{:S(2)}, u32[]{:S(2)}) collective-permute-start(bf16[3,1,16,128]{3,2,1,0:T(8,128)(2,1)S(1)} %pad_maximum_fusion.10), channel_id=1, source_target_pairs={{1,0},{2,1},{3,2},{5,4},{6,5},{7,6},{9,8},{10,9},{11,10},{13,12},{... | collective-permute-start | bytes 36872 | tf_op jit(solution)/shard_map/ppermute | solution.py:18
  64.6 5.4 %collective-permute-start.10 = (bf16[3,1,16,128]{3,2,1,0:T(8,128)(2,1)S(1)}, bf16[3,1,16,128]{3,2,1,0:T(8,128)(2,1)S(1)}, u32[]{:S(2)}, u32[]{:S(2)}) collective-permute-start(bf16[3,1,16,128]{3,2,1,0:T(8,128)(2,1)S(1)} %pad_maximum_fusion.10), channel_id=1, source_target_pairs={{0,1},{1,2},{2,3},{4,5},{5,6},{6,7},{8,9},{9,10},{10,11},{12,13},{... | collective-permute-start | bytes 36872 | tf_op jit(solution)/shard_map/ppermute | solution.py:17
  74.6 9.9 %collective-permute-start.13 = (bf16[1,1,16,128]{3,2,1,0:T(8,128)(2,1)S(1)}, bf16[1,1,16,128]{3,2,1,0:T(8,128)(2,1)S(1)}, u32[]{:S(2)}, u32[]{:S(2)}) collective-permute-start(bf16[1,1,16,128]{3,2,1,0:T(8,128)(2,1)S(1)} %get-tuple-element.14), channel_id=1, source_target_pairs={{4,0},{8,4},{12,8},{16,12},{20,16},{24,20},{28,24},{32,28},{36,32}... | collective-permute-start | bytes 12296 | tf_op jit(solution)/shard_map/ppermute | solution.py:18
  82.5 3.1 %collective-permute-start.12 = (bf16[1,1,16,128]{3,2,1,0:T(8,128)(2,1)S(1)}, bf16[1,1,16,128]{3,2,1,0:T(8,128)(2,1)S(1)}, u32[]{:S(2)}, u32[]{:S(2)}) collective-permute-start(bf16[1,1,16,128]{3,2,1,0:T(8,128)(2,1)S(1)} %get-tuple-element.14), channel_id=1, source_target_pairs={{0,4},{4,8},{8,12},{12,16},{16,20},{20,24},{24,28},{28,32},{32,36}... | collective-permute-start | bytes 12296 | tf_op jit(solution)/shard_map/ppermute | solution.py:17
  85.6 5.8 %collective-permute-start.15 = (bf16[3,1,16,128]{3,2,1,0:T(8,128)(2,1)S(1)}, bf16[3,1,16,128]{3,2,1,0:T(8,128)(2,1)S(1)}, u32[]{:S(2)}, u32[]{:S(2)}) collective-permute-start(bf16[3,1,16,128]{3,2,1,0:T(8,128)(2,1)S(1)} %pad_maximum_fusion.11), channel_id=1, source_target_pairs={{1,0},{2,1},{3,2},{5,4},{6,5},{7,6},{9,8},{10,9},{11,10},{13,12},{... | collective-permute-start | bytes 36872 | tf_op jit(solution)/shard_map/ppermute | solution.py:18
  86.9 5.4 %collective-permute-start.14 = (bf16[3,1,16,128]{3,2,1,0:T(8,128)(2,1)S(1)}, bf16[3,1,16,128]{3,2,1,0:T(8,128)(2,1)S(1)}, u32[]{:S(2)}, u32[]{:S(2)}) collective-permute-start(bf16[3,1,16,128]{3,2,1,0:T(8,128)(2,1)S(1)} %pad_maximum_fusion.11), channel_id=1, source_target_pairs={{0,1},{1,2},{2,3},{4,5},{5,6},{6,7},{8,9},{9,10},{10,11},{12,13},{... | collective-permute-start | bytes 36872 | tf_op jit(solution)/shard_map/ppermute | solution.py:17
  96.9 9.9 %collective-permute-start.17 = (bf16[1,1,16,128]{3,2,1,0:T(8,128)(2,1)S(1)}, bf16[1,1,16,128]{3,2,1,0:T(8,128)(2,1)S(1)}, u32[]{:S(2)}, u32[]{:S(2)}) collective-permute-start(bf16[1,1,16,128]{3,2,1,0:T(8,128)(2,1)S(1)} %get-tuple-element.12), channel_id=1, source_target_pairs={{4,0},{8,4},{12,8},{16,12},{20,16},{24,20},{28,24},{32,28},{36,32}... | collective-permute-start | bytes 12296 | tf_op jit(solution)/shard_map/ppermute | solution.py:18
  104.8 3.1 %collective-permute-start.16 = (bf16[1,1,16,128]{3,2,1,0:T(8,128)(2,1)S(1)}, bf16[1,1,16,128]{3,2,1,0:T(8,128)(2,1)S(1)}, u32[]{:S(2)}, u32[]{:S(2)}) collective-permute-start(bf16[1,1,16,128]{3,2,1,0:T(8,128)(2,1)S(1)} %get-tuple-element.12), channel_id=1, source_target_pairs={{0,4},{4,8},{8,12},{12,16},{16,20},{20,24},{24,28},{28,32},{32,36}... | collective-permute-start | bytes 12296 | tf_op jit(solution)/shard_map/ppermute | solution.py:17
  107.9 5.8 %collective-permute-start.19 = (bf16[3,1,16,128]{3,2,1,0:T(8,128)(2,1)S(1)}, bf16[3,1,16,128]{3,2,1,0:T(8,128)(2,1)S(1)}, u32[]{:S(2)}, u32[]{:S(2)}) collective-permute-start(bf16[3,1,16,128]{3,2,1,0:T(8,128)(2,1)S(1)} %pad_maximum_fusion.12), channel_id=1, source_target_pairs={{1,0},{2,1},{3,2},{5,4},{6,5},{7,6},{9,8},{10,9},{11,10},{13,12},{... | collective-permute-start | bytes 36872 | tf_op jit(solution)/shard_map/ppermute | solution.py:18
  109.2 5.4 %collective-permute-start.18 = (bf16[3,1,16,128]{3,2,1,0:T(8,128)(2,1)S(1)}, bf16[3,1,16,128]{3,2,1,0:T(8,128)(2,1)S(1)}, u32[]{:S(2)}, u32[]{:S(2)}) collective-permute-start(bf16[3,1,16,128]{3,2,1,0:T(8,128)(2,1)S(1)} %pad_maximum_fusion.12), channel_id=1, source_target_pairs={{0,1},{1,2},{2,3},{4,5},{5,6},{6,7},{8,9},{9,10},{10,11},{12,13},{... | collective-permute-start | bytes 36872 | tf_op jit(solution)/shard_map/ppermute | solution.py:17
  119.1 9.9 %collective-permute-start.21 = (bf16[1,1,16,128]{3,2,1,0:T(8,128)(2,1)S(1)}, bf16[1,1,16,128]{3,2,1,0:T(8,128)(2,1)S(1)}, u32[]{:S(2)}, u32[]{:S(2)}) collective-permute-start(bf16[1,1,16,128]{3,2,1,0:T(8,128)(2,1)S(1)} %get-tuple-element.10), channel_id=1, source_target_pairs={{4,0},{8,4},{12,8},{16,12},{20,16},{24,20},{28,24},{32,28},{36,32}... | collective-permute-start | bytes 12296 | tf_op jit(solution)/shard_map/ppermute | solution.py:18
  127.1 3.1 %collective-permute-start.20 = (bf16[1,1,16,128]{3,2,1,0:T(8,128)(2,1)S(1)}, bf16[1,1,16,128]{3,2,1,0:T(8,128)(2,1)S(1)}, u32[]{:S(2)}, u32[]{:S(2)}) collective-permute-start(bf16[1,1,16,128]{3,2,1,0:T(8,128)(2,1)S(1)} %get-tuple-element.10), channel_id=1, source_target_pairs={{0,4},{4,8},{8,12},{12,16},{16,20},{20,24},{24,28},{28,32},{32,36}... | collective-permute-start | bytes 12296 | tf_op jit(solution)/shard_map/ppermute | solution.py:17
  130.1 5.8 %collective-permute-start.23 = (bf16[3,1,16,128]{3,2,1,0:T(8,128)(2,1)S(1)}, bf16[3,1,16,128]{3,2,1,0:T(8,128)(2,1)S(1)}, u32[]{:S(2)}, u32[]{:S(2)}) collective-permute-start(bf16[3,1,16,128]{3,2,1,0:T(8,128)(2,1)S(1)} %pad_maximum_fusion.13), channel_id=1, source_target_pairs={{1,0},{2,1},{3,2},{5,4},{6,5},{7,6},{9,8},{10,9},{11,10},{13,12},{... | collective-permute-start | bytes 36872 | tf_op jit(solution)/shard_map/ppermute | solution.py:18
  131.4 5.4 %collective-permute-start.22 = (bf16[3,1,16,128]{3,2,1,0:T(8,128)(2,1)S(1)}, bf16[3,1,16,128]{3,2,1,0:T(8,128)(2,1)S(1)}, u32[]{:S(2)}, u32[]{:S(2)}) collective-permute-start(bf16[3,1,16,128]{3,2,1,0:T(8,128)(2,1)S(1)} %pad_maximum_fusion.13), channel_id=1, source_target_pairs={{0,1},{1,2},{2,3},{4,5},{5,6},{6,7},{8,9},{9,10},{10,11},{12,13},{... | collective-permute-start | bytes 36872 | tf_op jit(solution)/shard_map/ppermute | solution.py:17
  141.4 9.9 %collective-permute-start.25 = (bf16[1,1,16,128]{3,2,1,0:T(8,128)(2,1)S(1)}, bf16[1,1,16,128]{3,2,1,0:T(8,128)(2,1)S(1)}, u32[]{:S(2)}, u32[]{:S(2)}) collective-permute-start(bf16[1,1,16,128]{3,2,1,0:T(8,128)(2,1)S(1)} %get-tuple-element.8), channel_id=1, source_target_pairs={{4,0},{8,4},{12,8},{16,12},{20,16},{24,20},{28,24},{32,28},{36,32}... | collective-permute-start | bytes 12296 | tf_op jit(solution)/shard_map/ppermute | solution.py:18
  149.4 3.1 %collective-permute-start.24 = (bf16[1,1,16,128]{3,2,1,0:T(8,128)(2,1)S(1)}, bf16[1,1,16,128]{3,2,1,0:T(8,128)(2,1)S(1)}, u32[]{:S(2)}, u32[]{:S(2)}) collective-permute-start(bf16[1,1,16,128]{3,2,1,0:T(8,128)(2,1)S(1)} %get-tuple-element.8), channel_id=1, source_target_pairs={{0,4},{4,8},{8,12},{12,16},{16,20},{20,24},{24,28},{28,32},{32,36}... | collective-permute-start | bytes 12296 | tf_op jit(solution)/shard_map/ppermute | solution.py:17
  152.5 5.8 %collective-permute-start.27 = (bf16[3,1,16,128]{3,2,1,0:T(8,128)(2,1)S(1)}, bf16[3,1,16,128]{3,2,1,0:T(8,128)(2,1)S(1)}, u32[]{:S(2)}, u32[]{:S(2)}) collective-permute-start(bf16[3,1,16,128]{3,2,1,0:T(8,128)(2,1)S(1)} %pad_maximum_fusion.14), channel_id=1, source_target_pairs={{1,0},{2,1},{3,2},{5,4},{6,5},{7,6},{9,8},{10,9},{11,10},{13,12},{... | collective-permute-start | bytes 36872 | tf_op jit(solution)/shard_map/ppermute | solution.py:18
  153.7 5.4 %collective-permute-start.26 = (bf16[3,1,16,128]{3,2,1,0:T(8,128)(2,1)S(1)}, bf16[3,1,16,128]{3,2,1,0:T(8,128)(2,1)S(1)}, u32[]{:S(2)}, u32[]{:S(2)}) collective-permute-start(bf16[3,1,16,128]{3,2,1,0:T(8,128)(2,1)S(1)} %pad_maximum_fusion.14), channel_id=1, source_target_pairs={{0,1},{1,2},{2,3},{4,5},{5,6},{6,7},{8,9},{9,10},{10,11},{12,13},{... | collective-permute-start | bytes 36872 | tf_op jit(solution)/shard_map/ppermute | solution.py:17
  163.8 9.9 %collective-permute-start.29 = (bf16[1,1,16,128]{3,2,1,0:T(8,128)(2,1)S(1)}, bf16[1,1,16,128]{3,2,1,0:T(8,128)(2,1)S(1)}, u32[]{:S(2)}, u32[]{:S(2)}) collective-permute-start(bf16[1,1,16,128]{3,2,1,0:T(8,128)(2,1)S(1)} %get-tuple-element.6), channel_id=1, source_target_pairs={{4,0},{8,4},{12,8},{16,12},{20,16},{24,20},{28,24},{32,28},{36,32}... | collective-permute-start | bytes 12296 | tf_op jit(solution)/shard_map/ppermute | solution.py:18
  171.7 3.1 %collective-permute-start.28 = (bf16[1,1,16,128]{3,2,1,0:T(8,128)(2,1)S(1)}, bf16[1,1,16,128]{3,2,1,0:T(8,128)(2,1)S(1)}, u32[]{:S(2)}, u32[]{:S(2)}) collective-permute-start(bf16[1,1,16,128]{3,2,1,0:T(8,128)(2,1)S(1)} %get-tuple-element.6), channel_id=1, source_target_pairs={{0,4},{4,8},{8,12},{12,16},{16,20},{20,24},{24,28},{28,32},{32,36}... | collective-permute-start | bytes 12296 | tf_op jit(solution)/shard_map/ppermute | solution.py:17
  174.8 5.8 %collective-permute-start.31 = (bf16[3,1,16,128]{3,2,1,0:T(8,128)(2,1)S(1)}, bf16[3,1,16,128]{3,2,1,0:T(8,128)(2,1)S(1)}, u32[]{:S(2)}, u32[]{:S(2)}) collective-permute-start(bf16[3,1,16,128]{3,2,1,0:T(8,128)(2,1)S(1)} %pad_maximum_fusion.15), channel_id=1, source_target_pairs={{1,0},{2,1},{3,2},{5,4},{6,5},{7,6},{9,8},{10,9},{11,10},{13,12},{... | collective-permute-start | bytes 36872 | tf_op jit(solution)/shard_map/ppermute | solution.py:18
  176.1 5.4 %collective-permute-start.30 = (bf16[3,1,16,128]{3,2,1,0:T(8,128)(2,1)S(1)}, bf16[3,1,16,128]{3,2,1,0:T(8,128)(2,1)S(1)}, u32[]{:S(2)}, u32[]{:S(2)}) collective-permute-start(bf16[3,1,16,128]{3,2,1,0:T(8,128)(2,1)S(1)} %pad_maximum_fusion.15), channel_id=1, source_target_pairs={{0,1},{1,2},{2,3},{4,5},{5,6},{6,7},{8,9},{9,10},{10,11},{12,13},{... | collective-permute-start | bytes 36872 | tf_op jit(solution)/shard_map/ppermute | solution.py:17
  (1 other events, 28.0 us)
where the time goes:
time: 304 us; the launch traced here: 303 us
  starting transfers between devices  122 us (40%)
  blocking collectives  113 us (37%)
  matrix products  26 us (9%)
  waiting for transfers between devices  22.5 us (7%)
  local copies, waits for them, and re-layouts  9.16 us (3%)
  other arithmetic  8.9 us (3%)
    psum x1, blocking collectives, on_device(): gram = lax.psum(partial_gram, ('dom', 'sub')) / total_rows  113 us
    ppermute x16, starting transfers between devices, extended(): after = lax.ppermute(initial, axis, down)  69.3 us
    ppermute x16, starting transfers between devices, extended(): before = lax.ppermute(last, axis, up)  53.1 us
    dot_general x8, matrix products, apply_matrix(): jnp.einsum('rnij,rnj->ri', local_blocks, picked, preferred_element_type=j...  25.8 us
    ppermute x16, waiting for transfers between devices, extended(): before = lax.ppermute(last, axis, up)  22.4 us
  transfers between devices with their start and end apart: 32, of which 16 were waited for; matrix products, arithmetic and copies ran while one was open for 1% of the time, Pallas kernels for 0%

commit v1 on v0

v1 whole, which is shorter than its diff:
```python
import functools

import jax
import jax.numpy as jnp
from jax import lax
from jax.experimental import pallas as pl
from jax.experimental.pallas import tpu as pltpu
from jax.sharding import Mesh, PartitionSpec as P

S = 8
S1 = 9
NB = 7
BR = 16
BLK = 128
SUBS = 4
NY, NZ, NCORE = 8, 12, 2
DOMS = NY * NZ * NCORE
CHIPS = DOMS // NCORE
DOM = ("y", "z", "core")
ALL = DOM + ("sub",)
VMEM = pl.BlockSpec(memory_space=pltpu.VMEM)
PARAMS = pltpu.CompilerParams(vmem_limit_bytes=16 * 1024 * 1024)


def outer_groups():
    return [
        [(d % DOMS) * SUBS + s for d in (2 * c - 1, 2 * c) for s in range(SUBS)]
        for c in range(CHIPS)
    ]


def pool_rows(columns):
    d = (lax.axis_index("y") * NZ + lax.axis_index("z")) * NCORE + lax.axis_index("core")
    s = lax.axis_index("sub")
    core = lax.axis_index("core")
    slot, row = columns // BR, columns % BR
    a, b = slot // 3 - 1, slot % 3 - 1
    chip_core = core + a
    member = jnp.where(core == 0, jnp.where(a < 0, 0, 1), jnp.where(a > 0, 1, 0))
    held = chip_core % NCORE
    nd, ns = d + a, s + b
    inside = (nd >= 0) & (nd < DOMS) & (ns >= 0) & (ns < SUBS)
    index = ((member * SUBS + ns) * NCORE + held) * BR + row
    return jnp.where(inside, index, -1)


def product(k, pool_ref, hot_ref, blocks_ref, v_ref, shifts_ref):
    pool = pool_ref[...].reshape(-1, BLK)
    picked = jnp.dot(hot_ref[...], pool, preferred_element_type=jnp.float32).astype(jnp.bfloat16)
    parts = [picked[n * BR:(n + 1) * BR] for n in range(NB)]
    wide = [jnp.concatenate(parts[n:n + 2], axis=1) for n in range(0, NB, 2)]
    lane = lax.broadcasted_iota(jnp.int32, (BR, BLK), 0)
    total = jnp.zeros((BR, BLK), jnp.float32)
    for r in range(BR):
        acc = None
        for p, x in enumerate(wide):
            rows = [blocks_ref[r, n] for n in range(2 * p, min(2 * p + 2, NB))]
            block = jnp.concatenate(rows, axis=1)
            term = lax.dot_general(x, block, (((1,), (1,)), ((), ())), preferred_element_type=jnp.float32)
            acc = term if acc is None else acc + term
        total = jnp.where(lane == r, acc, total)
    return total - shifts_ref[0:1, k:k + 1] * v_ref[...]


def step_kernel(k, pool_ref, hot_ref, blocks_ref, v_ref, shifts_ref, out_ref, rounded_ref):
    new = product(k, pool_ref, hot_ref, blocks_ref, v_ref, shifts_ref)
    out_ref[...] = new
    rounded_ref[...] = new.astype(jnp.bfloat16)


def last_kernel(pool_ref, hot_ref, blocks_ref, shifts_ref, *refs):
    ins, basis_ref, gram_ref = refs[:S], refs[S], refs[S + 1]
    vectors = [ref[...] for ref in ins]
    new = product(S - 1, pool_ref, hot_ref, blocks_ref, ins[-1], shifts_ref)
    vectors.append(new)
    for i, v in enumerate(vectors):
        basis_ref[i] = v
    lane = lax.broadcasted_iota(jnp.int32, (S, BLK), 1)
    sub = lax.broadcasted_iota(jnp.int32, (S, BLK), 0)
    tile = jnp.zeros((S, BLK), jnp.float32)

    def rows(i, j):
        prod = vectors[i] * vectors[j]
        return jnp.sum(prod, axis=0, keepdims=True)

    for i in range(S1):
        stack = jnp.zeros((S, BLK), jnp.float32)
        for j in range(min(i + 1, S)):
            stack = jnp.where(sub == j, rows(i, j), stack)
        tile = jnp.where(lane == i, jnp.sum(stack, axis=1, keepdims=True), tile)
    corner = jnp.sum(rows(S, S), axis=1, keepdims=True)
    gram_ref[...] = jnp.where((lane == S1) & (sub == 0), corner, tile)


def factor_kernel(rows_total, parts_ref, out_ref):
    tile = jnp.sum(parts_ref[...], axis=0) / rows_total
    size = 16
    pad = jnp.concatenate([tile, jnp.zeros((size - S, BLK), jnp.float32)], axis=0)
    lane = lax.broadcasted_iota(jnp.int32, (size, BLK), 1)
    sub = lax.broadcasted_iota(jnp.int32, (size, BLK), 0)
    upper = jnp.where((sub == S) & (lane == S), pad[0:1, S1:S1 + 1], jnp.where((lane >= sub) & (lane < S1), pad, 0.0))
    full = upper
    result = jnp.zeros((size, BLK), jnp.float32)
    for k in range(S1):
        row = full[k:k + 1, :]
        pivot = row[:, k:k + 1]
        root = jnp.sqrt(pivot)
        line = jnp.where(lane[0:1] >= k, row, 0.0) / root
        result = jnp.where(sub == k, line, result)
        spread = jnp.broadcast_to(line, (size, BLK))
        down = jnp.sum(jnp.where(lane == sub, spread, 0.0), axis=1, keepdims=True)
        full = full - down * line
    out_ref[...] = result[0:S1, 0:S1]


def step(k, pool, hot, blocks, v, shifts):
    return pl.pallas_call(
        functools.partial(step_kernel, k),
        out_shape=(jax.ShapeDtypeStruct((BR, BLK), jnp.float32), jax.ShapeDtypeStruct((BR, BLK), jnp.bfloat16)),
        in_specs=[VMEM] * 5,
        out_specs=(VMEM, VMEM),
        compiler_params=PARAMS,
        name="step",
    )(pool, hot, blocks, v, shifts)


def last_step(pool, hot, blocks, shifts, vectors):
    return pl.pallas_call(
        last_kernel,
        out_shape=(jax.ShapeDtypeStruct((S1, BR, BLK), jnp.float32), jax.ShapeDtypeStruct((S, BLK), jnp.float32)),
        in_specs=[VMEM] * (4 + S),
        out_specs=(VMEM, VMEM),
        compiler_params=PARAMS,
        name="last",
    )(pool, hot, blocks, shifts, *vectors)


def to_all(value, axes, peers):
    return lax.all_to_all(jnp.broadcast_to(value, (peers,) + value.shape), axes, 0, 0)


def on_device(groups, start_vector, blocks, columns, shifts):
    blocks = blocks[0, 0]
    rows = pool_rows(columns[0, 0]).T.reshape(NB * BR, 1)
    pool_size = len(groups[0]) * NCORE * BR
    hot = (rows == lax.broadcasted_iota(jnp.int32, (NB * BR, pool_size), 1)).astype(jnp.bfloat16)
    shifts = shifts.reshape(1, S)
    v = start_vector[0, 0]
    rounded = v.astype(jnp.bfloat16)
    vectors = [v]
    for k in range(S):
        chip = lax.all_gather(rounded, "core")
        chip = jnp.broadcast_to(chip, (len(groups[0]),) + chip.shape)
        pool = lax.all_to_all(chip, ALL, 0, 0, axis_index_groups=groups)
        if k < S - 1:
            v, rounded = step(k, pool, hot, blocks, v, shifts)
            vectors.append(v)
    basis, gram = last_step(pool, hot, blocks, shifts, vectors)
    gram = jnp.sum(to_all(gram, ("y", "sub"), NY * SUBS), axis=0)
    parts = to_all(gram, ("z", "core"), NZ * NCORE)
    factor = pl.pallas_call(
        functools.partial(factor_kernel, DOMS * SUBS * BR * BLK),
        out_shape=jax.ShapeDtypeStruct((S1, S1), jnp.float32),
        in_specs=[VMEM],
        out_specs=VMEM,
        name="factor",
    )(parts)
    return basis.reshape(S1, 1, 1, BR, BLK), factor


def solution(mesh):
    split = Mesh(mesh.devices.reshape(NY, NZ, NCORE, SUBS), ALL)
    return jax.shard_map(
        functools.partial(on_device, outer_groups()),
        mesh=split,
        in_specs=(P(DOM, "sub"), P(DOM, "sub"), P(DOM, "sub"), P()),
        out_specs=(P(None, DOM, "sub"), P()),
        check_vma=False,
    )
```

time: 304 us -> 172 us (0.57)
  the two profiles are of different devices: /device:TPU:33 before, /device:TPU:1 now
where the time goes in v1:
time: 172 us; the launch traced here: 171 us
  blocking collectives  143 us (83%)
  Pallas kernels  13.2 us (8%)
  waiting for transfers between devices  4.79 us (3%)
  local copies, waits for them, and re-layouts  4.21 us (2%)
  starting transfers between devices  3.35 us (2%)
    all_to_all x7, blocking collectives, on_device(): pool = lax.all_to_all(chip, ALL, 0, 0, axis_index_groups=groups)  59.1 us
    all_gather x8, blocking collectives, on_device(): chip = lax.all_gather(rounded, 'core')  50.5 us
    all_to_all x2, blocking collectives, to_all(): lax.all_to_all(jnp.broadcast_to(value, (peers,) + value.shape), axes, 0, 0)  33.4 us
    pallas_call x7, Pallas kernels, step(): pl.pallas_call(functools.partial(step_kernel, k), out_shape=(jax.ShapeDty...  8.39 us
    all_to_all x1, waiting for transfers between devices, on_device(): pool = lax.all_to_all(chip, ALL, 0, 0, axis_index_groups=groups)  4.79 us
  transfers between devices with their start and end apart: 1, of which 1 were waited for; matrix products, arithmetic and copies ran while one was open for 1% of the time, Pallas kernels for 0%

profile of v1, /device:TPU:1, one launch (start us, length us, event | category | flops | bytes accessed | tf_op | source)
XLA Modules:
  0.0 171.0 jit_solution(1003965814702108994)
XLA Ops:
  0.6 0.7 convert_element_type.16
  1.3 12.0 %all-gather = bf16[2,1,16,128]{3,2,1,0:T(8,128)(2,1)S(1)} all-gather(bf16[1,1,16,128]{3,2,1,0:T(8,128)(2,1)S(1)} %convert_element_type.16), channel_id=2, replica_groups=mesh['y'=8,'z'=12,'core'=2,'sub'=4] {'core'}, dimensions={0}, use_global_device_ids=true | all-gather | bytes 12288 | tf_op jit(solution)/shard_map/all_gather | solution.py:152
  14.0 3.4 %all-to-all-start = ((bf16[8,2,16,128]{3,2,1,0:T(8,128)(2,1)}), bf16[8,2,16,128]{3,2,1,0:T(8,128)(2,1)S(1)}, u32[]{:S(2)}, u32[]{:S(2)}) async-start(bf16[8,2,16,128]{3,2,1,0:T(8,128)(2,1)} %broadcast_in_dim.38), calls=%async_computation | async-start | bytes 131072 | tf_op jit(solution)/shard_map/all_to_all | solution.py:154
  17.3 0.7 fusion.9
  18.2 4.8 %all-to-all-done.pool_ref = bf16[8,2,16,128]{3,2,1,0:T(8,128)(2,1)S(1)} async-done(((bf16[8,2,16,128]{3,2,1,0:T(8,128)(2,1)}), bf16[8,2,16,128]{3,2,1,0:T(8,128)(2,1)S(1)}, u32[]{:S(2)}, u32[]{:S(2)}) %all-to-all-start) | async-done | bytes 65568 | tf_op jit(solution)/shard_map/all_to_all | solution.py:154
  23.0 2.0 %copy-done = bf16[1,1,16,7,128,128]{5,4,3,2,1,0:T(8,128)(2,1)S(1)} copy-done((bf16[1,1,16,7,128,128]{5,4,3,2,1,0:T(8,128)(2,1)S(1)}, bf16[1,1,16,7,128,128]{5,4,3,2,1,0:T(8,128)(2,1)}, u32[]{:S(2)}) %copy-start) | copy-done | bytes 3670040
  25.1 0.7 copy-done.2
  26.4 1.2 step.7
  27.6 8.0 %all-gather.1 = bf16[32,128]{1,0:T(8,128)(2,1)S(1)} all-gather(bf16[16,128]{1,0:T(8,128)(2,1)S(1)} %get-tuple-element.18), channel_id=3, replica_groups=mesh['y'=8,'z'=12,'core'=2,'sub'=4] {'core'}, dimensions={0}, use_global_device_ids=true | all-gather | bytes 12288 | tf_op jit(solution)/shard_map/all_gather | solution.py:152
  35.7 8.4 %all_to_all.50.pool_ref = bf16[8,2,16,128]{3,2,1,0:T(8,128)(2,1)S(1)} all-to-all(bf16[8,2,16,128]{3,2,1,0:T(8,128)(2,1)S(1)} %broadcast_in_dim.39), channel_id=1, replica_groups={{764,765,766,767,0,1,2,3},{4,5,6,7,8,9,10,11},{12,13,14,15,16,17,18,19}..., dimensions={0} | all-to-all | bytes 131072 | tf_op jit(solution)/shard_map/all_to_all | solution.py:154
  44.1 1.2 step.8
  45.3 5.1 %all-gather.2 = bf16[32,128]{1,0:T(8,128)(2,1)S(1)} all-gather(bf16[16,128]{1,0:T(8,128)(2,1)S(1)} %get-tuple-element.20), channel_id=4, replica_groups=mesh['y'=8,'z'=12,'core'=2,'sub'=4] {'core'}, dimensions={0}, use_global_device_ids=true | all-gather | bytes 12288 | tf_op jit(solution)/shard_map/all_gather | solution.py:152
  50.4 8.4 %all_to_all.51.pool_ref = bf16[8,2,16,128]{3,2,1,0:T(8,128)(2,1)S(1)} all-to-all(bf16[8,2,16,128]{3,2,1,0:T(8,128)(2,1)S(1)} %broadcast_in_dim.40), channel_id=1, replica_groups={{764,765,766,767,0,1,2,3},{4,5,6,7,8,9,10,11},{12,13,14,15,16,17,18,19}..., dimensions={0} | all-to-all | bytes 131072 | tf_op jit(solution)/shard_map/all_to_all | solution.py:154
  58.9 1.2 step.9
  60.1 5.1 %all-gather.3 = bf16[32,128]{1,0:T(8,128)(2,1)S(1)} all-gather(bf16[16,128]{1,0:T(8,128)(2,1)S(1)} %get-tuple-element.22), channel_id=5, replica_groups=mesh['y'=8,'z'=12,'core'=2,'sub'=4] {'core'}, dimensions={0}, use_global_device_ids=true | all-gather | bytes 12288 | tf_op jit(solution)/shard_map/all_gather | solution.py:152
  65.2 8.4 %all_to_all.52.pool_ref = bf16[8,2,16,128]{3,2,1,0:T(8,128)(2,1)S(1)} all-to-all(bf16[8,2,16,128]{3,2,1,0:T(8,128)(2,1)S(1)} %broadcast_in_dim.41), channel_id=1, replica_groups={{764,765,766,767,0,1,2,3},{4,5,6,7,8,9,10,11},{12,13,14,15,16,17,18,19}..., dimensions={0} | all-to-all | bytes 131072 | tf_op jit(solution)/shard_map/all_to_all | solution.py:154
  73.6 1.2 step.10
  74.8 5.1 %all-gather.4 = bf16[32,128]{1,0:T(8,128)(2,1)S(1)} all-gather(bf16[16,128]{1,0:T(8,128)(2,1)S(1)} %get-tuple-element.24), channel_id=6, replica_groups=mesh['y'=8,'z'=12,'core'=2,'sub'=4] {'core'}, dimensions={0}, use_global_device_ids=true | all-gather | bytes 12288 | tf_op jit(solution)/shard_map/all_gather | solution.py:152
  79.9 8.4 %all_to_all.53.pool_ref = bf16[8,2,16,128]{3,2,1,0:T(8,128)(2,1)S(1)} all-to-all(bf16[8,2,16,128]{3,2,1,0:T(8,128)(2,1)S(1)} %broadcast_in_dim.42), channel_id=1, replica_groups={{764,765,766,767,0,1,2,3},{4,5,6,7,8,9,10,11},{12,13,14,15,16,17,18,19}..., dimensions={0} | all-to-all | bytes 131072 | tf_op jit(solution)/shard_map/all_to_all | solution.py:154
  88.4 1.2 step.11
  89.6 5.1 %all-gather.5 = bf16[32,128]{1,0:T(8,128)(2,1)S(1)} all-gather(bf16[16,128]{1,0:T(8,128)(2,1)S(1)} %get-tuple-element.26), channel_id=7, replica_groups=mesh['y'=8,'z'=12,'core'=2,'sub'=4] {'core'}, dimensions={0}, use_global_device_ids=true | all-gather | bytes 12288 | tf_op jit(solution)/shard_map/all_gather | solution.py:152
  94.7 8.4 %all_to_all.54.pool_ref = bf16[8,2,16,128]{3,2,1,0:T(8,128)(2,1)S(1)} all-to-all(bf16[8,2,16,128]{3,2,1,0:T(8,128)(2,1)S(1)} %broadcast_in_dim.43), channel_id=1, replica_groups={{764,765,766,767,0,1,2,3},{4,5,6,7,8,9,10,11},{12,13,14,15,16,17,18,19}..., dimensions={0} | all-to-all | bytes 131072 | tf_op jit(solution)/shard_map/all_to_all | solution.py:154
  103.1 1.2 step.12
  104.4 5.1 %all-gather.6 = bf16[32,128]{1,0:T(8,128)(2,1)S(1)} all-gather(bf16[16,128]{1,0:T(8,128)(2,1)S(1)} %get-tuple-element.28), channel_id=8, replica_groups=mesh['y'=8,'z'=12,'core'=2,'sub'=4] {'core'}, dimensions={0}, use_global_device_ids=true | all-gather | bytes 12288 | tf_op jit(solution)/shard_map/all_gather | solution.py:152
  109.5 8.4 %all_to_all.55.pool_ref = bf16[8,2,16,128]{3,2,1,0:T(8,128)(2,1)S(1)} all-to-all(bf16[8,2,16,128]{3,2,1,0:T(8,128)(2,1)S(1)} %broadcast_in_dim.44), channel_id=1, replica_groups={{764,765,766,767,0,1,2,3},{4,5,6,7,8,9,10,11},{12,13,14,15,16,17,18,19}..., dimensions={0} | all-to-all | bytes 131072 | tf_op jit(solution)/shard_map/all_to_all | solution.py:154
  117.9 1.2 step.13
  119.1 5.1 %all-gather.7 = bf16[32,128]{1,0:T(8,128)(2,1)S(1)} all-gather(bf16[16,128]{1,0:T(8,128)(2,1)S(1)} %get-tuple-element.30), channel_id=9, replica_groups=mesh['y'=8,'z'=12,'core'=2,'sub'=4] {'core'}, dimensions={0}, use_global_device_ids=true | all-gather | bytes 12288 | tf_op jit(solution)/shard_map/all_gather | solution.py:152
  124.2 8.4 %all_to_all.56.pool_ref = bf16[8,2,16,128]{3,2,1,0:T(8,128)(2,1)S(1)} all-to-all(bf16[8,2,16,128]{3,2,1,0:T(8,128)(2,1)S(1)} %broadcast_in_dim.45), channel_id=1, replica_groups={{764,765,766,767,0,1,2,3},{4,5,6,7,8,9,10,11},{12,13,14,15,16,17,18,19}..., dimensions={0} | all-to-all | bytes 131072 | tf_op jit(solution)/shard_map/all_to_all | solution.py:154
  132.7 2.0 %last.1 = (f32[9,16,128]{2,1,0:T(8,128)}, f32[8,128]{1,0:T(8,128)S(1)}) custom-call(bf16[8,2,16,128]{3,2,1,0:T(8,128)(2,1)S(1)} %all_to_all.56.pool_ref, bf16[112,256]{1,0:T(8,128)(2,1)S(1)} %fusion.hot_ref, bf16[16,7,128,128]{3,2,1,0:T(8,128)(2,1)S(1)} %bitcast.41, f32[1,8]{1,0:T(1,128)S(1)} %bitcast.51, f32[16,128]{1,0:T(8,128)S(1)} %bitcast.43, ...), custom_call_target="tpu_custom_call" | custom-call | tf_op jit(solution)/shard_map/last/pallas_call | solution.py:128
  134.6 13.9 %all_to_all.57 = f32[32,8,128]{2,1,0:T(8,128)S(1)} all-to-all(f32[32,8,128]{2,1,0:T(8,128)S(1)} %broadcast_in_dim.46), channel_id=1, replica_groups=mesh['y'=8,'z'=12,'core'=2,'sub'=4] {'y','sub'}, dimensions={0} | all-to-all | bytes 262144 | tf_op jit(solution)/shard_map/all_to_all | solution.py:139
  148.5 19.5 %all_to_all.58.parts_ref = f32[24,8,128]{2,1,0:T(8,128)} all-to-all(f32[24,8,128]{2,1,0:T(8,128)S(1)} %broadcast_in_dim.47), channel_id=1, replica_groups=mesh['y'=8,'z'=12,'core'=2,'sub'=4] {'z','core'}, dimensions={0} | all-to-all | bytes 196608 | tf_op jit(solution)/shard_map/all_to_all | solution.py:139
  168.1 2.9 %factor.1 = f32[9,9]{1,0:T(8,128)} custom-call(f32[24,8,128]{2,1,0:T(8,128)} %all_to_all.58.parts_ref), custom_call_target="tpu_custom_call" | custom-call | tf_op jit(solution)/shard_map/factor/pallas_call | solution.py:161
  (23 shorter events, 1.6 us)
Async XLA Ops:
  14.0 9.1 %all-to-all-start = ((bf16[8,2,16,128]{3,2,1,0:T(8,128)(2,1)}), bf16[8,2,16,128]{3,2,1,0:T(8,128)(2,1)S(1)}, u32[]{:S(2)}, u32[]{:S(2)}) async-start(bf16[8,2,16,128]{3,2,1,0:T(8,128)(2,1)} %broadcast_in_dim.38), calls=%async_computation | async-start | bytes 131072 | tf_op jit(solution)/shard_map/all_to_all | solution.py:154
  23.0 2.0 %copy-start = (bf16[1,1,16,7,128,128]{5,4,3,2,1,0:T(8,128)(2,1)S(1)}, bf16[1,1,16,7,128,128]{5,4,3,2,1,0:T(8,128)(2,1)}, u32[]{:S(2)}) copy-start(bf16[1,1,16,7,128,128]{5,4,3,2,1,0:T(8,128)(2,1)} %param.5) | copy-start | bytes 11010052
  25.1 0.7 copy-start.2
  25.8 0.7 copy-start.4
  26.4 17.7 %copy-start.1 = (bf16[1,1,16,7,128,128]{5,4,3,2,1,0:T(8,128)(2,1)S(1)}, bf16[1,1,16,7,128,128]{5,4,3,2,1,0:T(8,128)(2,1)}, u32[]{:S(2)}) copy-start(bf16[1,1,16,7,128,128]{5,4,3,2,1,0:T(8,128)(2,1)} %param.5) | copy-start | bytes 11010052
  73.6 29.5 %copy-start.5 = (f32[8]{0:T(128)S(1)}, f32[8]{0:T(128)}, u32[]{:S(2)}) copy-start(f32[8]{0:T(128)} %param.7) | copy-start | bytes 100
  103.1 29.5 %copy-start.3 = (f32[1,1,16,128]{3,2,1,0:T(8,128)S(1)}, f32[1,1,16,128]{3,2,1,0:T(8,128)}, u32[]{:S(2)}) copy-start(f32[1,1,16,128]{3,2,1,0:T(8,128)} %param.4) | copy-start | bytes 24580

commit v2 on v1

v2 whole, which is shorter than its diff:
```python
import functools

import jax
import jax.numpy as jnp
from jax import lax
from jax.experimental import pallas as pl
from jax.experimental.pallas import tpu as pltpu
from jax.sharding import Mesh, PartitionSpec as P

S = 8
S1 = 9
NB = 7
BR = 16
BLK = 128
MATRIX_ROWS = 6
SUBS = 4
NY, NZ, NCORE = 8, 12, 2
DOMS = NY * NZ * NCORE
CHIPS = DOMS // NCORE
PEERS = 2 * SUBS
POOL = PEERS * NCORE * BR
DOM = ("y", "z", "core")
ALL = DOM + ("sub",)
VMEM = pl.BlockSpec(memory_space=pltpu.VMEM)
PARAMS = pltpu.CompilerParams(vmem_limit_bytes=16 * 1024 * 1024)


def outer_groups():
    return [
        [(d % DOMS) * SUBS + s for d in (2 * c - 1, 2 * c) for s in range(SUBS)]
        for c in range(CHIPS)
    ]


def pool_rows(columns):
    core, s = lax.axis_index("core"), lax.axis_index("sub")
    d = (lax.axis_index("y") * NZ + lax.axis_index("z")) * NCORE + core
    slot, row = columns // BR, columns % BR
    a, b = slot // 3 - 1, slot % 3 - 1
    member = jnp.where((a < 0) & (core == 0), 0, jnp.where((a > 0) | (core == 0), 1, 0))
    held = (core + a + NCORE) % NCORE
    nd, ns = d + a, s + b
    inside = (nd >= 0) & (nd < DOMS) & (ns >= 0) & (ns < SUBS)
    index = ((member * SUBS + ns) * NCORE + held) * BR + row
    return jnp.where(inside, index, -1)


def one_hot(columns):
    rows = pool_rows(columns)
    place = lax.broadcasted_iota(jnp.int32, (BR, POOL), 1)
    return jnp.concatenate(
        [jnp.where(rows[:, n:n + 1] == place, 1.0, 0.0) for n in range(NB)], axis=0
    ).astype(jnp.bfloat16)


def product(k, pool_ref, hot_ref, blocks_ref, v_ref, packed_ref):
    pool = pool_ref[...].reshape(POOL, BLK)
    picked = jnp.dot(hot_ref[...], pool, preferred_element_type=jnp.float32)
    fields = [picked[n * BR:(n + 1) * BR] for n in range(NB)]
    line = jnp.concatenate(fields, axis=1).astype(jnp.bfloat16)
    row = lax.broadcasted_iota(jnp.int32, (BR, BLK), 0)
    lane = lax.broadcasted_iota(jnp.int32, (BLK, BLK), 1)
    by_matrix = jnp.zeros((BR, BLK), jnp.float32)
    by_vector = jnp.zeros((BLK, BLK), jnp.float32)

    def matrix_unit(r, total):
        block = jnp.concatenate([blocks_ref[r:r + 2, n].reshape(2 * BLK, BLK) for n in range(NB)], axis=1)
        pair = lax.dot_general(line, block, (((1,), (1,)), ((), ())), preferred_element_type=jnp.float32)
        return jnp.where(row == r, pair[:, :BLK], jnp.where(row == r + 1, pair[:, BLK:], total))

    def vector_unit(r, total):
        acc = None
        for n in range(NB):
            term = blocks_ref[r, n].astype(jnp.float32) * fields[n][r:r + 1]
            acc = term if acc is None else acc + term
        return jnp.where(lane == r, jnp.sum(acc, axis=1, keepdims=True), total)

    pairs, singles = list(range(0, MATRIX_ROWS, 2)), list(range(MATRIX_ROWS, BR))
    while pairs or singles:
        if pairs:
            by_matrix = matrix_unit(pairs.pop(0), by_matrix)
        if singles:
            by_vector = vector_unit(singles.pop(0), by_vector)
    image = jnp.where(row < MATRIX_ROWS, by_matrix, by_vector.T[:BR])
    return image - packed_ref[2 * BR:2 * BR + 1, k:k + 1] * v_ref[0:BR, :]


def spread_kernel(both_ref, packed_ref, blocks_ref, out_ref, hot_ref):
    both = both_ref[:, 0:BR, :].astype(jnp.bfloat16)
    for i in range(PEERS):
        out_ref[i] = both
    hot_ref[...] = one_hot(packed_ref[BR:2 * BR, :].astype(jnp.int32))


def step_kernel(k, pool_ref, hot_ref, blocks_ref, v_ref, packed_ref, out_ref, rounded_ref):
    new = product(k, pool_ref, hot_ref, blocks_ref, v_ref, packed_ref)
    out_ref[...] = new
    rounded_ref[...] = new.astype(jnp.bfloat16)


def inner(v, others):
    sub = lax.broadcasted_iota(jnp.int32, (S, BLK), 0)
    stack = jnp.zeros((S, BLK), jnp.float32)
    for j, w in enumerate(others):
        stack = jnp.where(sub == j, jnp.sum(v * w, axis=0, keepdims=True), stack)
    return jnp.sum(stack, axis=1, keepdims=True)


def last_kernel(pool_ref, hot_ref, blocks_ref, packed_ref, *refs):
    ins, out_ref, gram_ref = refs[:S], refs[S], refs[S + 1]
    new = product(S - 1, pool_ref, hot_ref, blocks_ref, ins[-1], packed_ref)
    out_ref[...] = new
    vectors = [ref[0:BR, :] for ref in ins] + [new]
    lane = lax.broadcasted_iota(jnp.int32, (S, BLK), 1)
    tile = jnp.zeros((S, BLK), jnp.float32)
    for i in range(S1):
        tile = jnp.where(lane == i, inner(vectors[i], vectors[:min(i + 1, S)]), tile)
    gram_ref[...] = jnp.where(lane == S1, inner(new, [new]), tile)


def factor_kernel(rows_total, parts_ref, *refs):
    out_ref, basis_ref = refs[S1], refs[S1 + 1]
    for i in range(S1):
        basis_ref[i] = refs[i][0:BR, :]
    tile = jnp.sum(parts_ref[...], axis=0) / rows_total
    spread = [jnp.broadcast_to(tile[:, i:i + 1], (S, BLK)) for i in range(S1 + 1)]
    a = {(j, i): jnp.broadcast_to(spread[i][j:j + 1], (S, BLK)) for i in range(S1) for j in range(min(i + 1, S))}
    a[S, S] = jnp.broadcast_to(spread[S1][0:1], (S, BLK))
    sub = lax.broadcasted_iota(jnp.int32, (S, BLK), 0)
    lane = lax.broadcasted_iota(jnp.int32, (S, BLK), 1)
    top = jnp.zeros((S, BLK), jnp.float32)
    bottom = None
    for k in range(S1):
        scale = lax.rsqrt(a[k, k])
        r = [a[k, i] * scale for i in range(k, S1)]
        whole = jnp.zeros((S, BLK), jnp.float32)
        for i in range(k, S1):
            whole = jnp.where(lane == i, r[i - k], whole)
            for j in range(k + 1, i + 1):
                a[j, i] = a[j, i] - r[j - k] * r[i - k]
        if k < S:
            top = jnp.where(sub == k, whole, top)
        else:
            bottom = whole
    out_ref[0:S, :] = top[:, 0:S1]
    out_ref[S:S1, :] = bottom[0:1, 0:S1]


def shape(*dims, dtype=jnp.float32):
    return jax.ShapeDtypeStruct(dims, dtype)


def spread(both, packed, blocks):
    return pl.pallas_call(
        spread_kernel,
        out_shape=(
            shape(PEERS, NCORE, BR, BLK, dtype=jnp.bfloat16),
            shape(NB * BR, POOL, dtype=jnp.bfloat16),
        ),
        in_specs=[VMEM] * 3,
        out_specs=(VMEM,) * 2,
        compiler_params=PARAMS,
        name="spread",
    )(both, packed, blocks)


def step(k, pool, hot, blocks, v, packed):
    return pl.pallas_call(
        functools.partial(step_kernel, k),
        out_shape=(shape(BR, BLK), shape(BR, BLK, dtype=jnp.bfloat16)),
        in_specs=[VMEM] * 5,
        out_specs=(VMEM, VMEM),
        compiler_params=PARAMS,
        name="step",
    )(pool, hot, blocks, v, packed)


def last_step(pool, hot, blocks, packed, vectors):
    return pl.pallas_call(
        last_kernel,
        out_shape=(shape(BR, BLK), shape(S, BLK)),
        in_specs=[VMEM] * (4 + S),
        out_specs=(VMEM, VMEM),
        compiler_params=PARAMS,
        name="last",
    )(pool, hot, blocks, packed, *vectors)


def to_all(value, axes, peers):
    return lax.all_to_all(jnp.broadcast_to(value, (peers,) + value.shape), axes, 0, 0)


def on_device(groups, start_vector, blocks, columns, shifts):
    blocks = blocks[0, 0]
    packed = jnp.concatenate([
        start_vector[0, 0],
        jnp.pad(columns[0, 0].astype(jnp.float32), ((0, 0), (0, BLK - NB))),
        jnp.pad(shifts.reshape(1, S), ((0, 7), (0, BLK - S))),
    ], axis=0)
    vectors = [packed]
    for k in range(S):
        if k == 0:
            chip, hot = spread(lax.all_gather(packed, "core"), packed, blocks)
        else:
            chip = lax.all_gather(rounded, "core")
            chip = jnp.broadcast_to(chip, (PEERS,) + chip.shape)
        pool = lax.all_to_all(chip, ALL, 0, 0, axis_index_groups=groups)
        if k < S - 1:
            v, rounded = step(k, pool, hot, blocks, vectors[-1], packed)
            vectors.append(v)
    v, gram = last_step(pool, hot, blocks, packed, vectors)
    gram = jnp.sum(to_all(gram, ("y", "sub"), NY * SUBS), axis=0)
    parts = to_all(gram, ("z", "core"), NZ * NCORE)
    factor, basis = pl.pallas_call(
        functools.partial(factor_kernel, DOMS * SUBS * BR * BLK),
        out_shape=(shape(S1, S1), shape(S1, BR, BLK)),
        in_specs=[VMEM] * (S1 + 1),
        out_specs=(VMEM, VMEM),
        compiler_params=PARAMS,
        name="factor",
    )(parts, *vectors, v)
    return basis.reshape(S1, 1, 1, BR, BLK), factor


def solution(mesh):
    split = Mesh(mesh.devices.reshape(NY, NZ, NCORE, SUBS), ALL)
    return jax.shard_map(
        functools.partial(on_device, outer_groups()),
        mesh=split,
        in_specs=(P(DOM, "sub"), P(DOM, "sub"), P(DOM, "sub"), P()),
        out_specs=(P(None, DOM, "sub"), P()),
        check_vma=False,
    )
```

time: 172 us -> 163 us (0.948)
  blocking collectives: 143 us -> 151 us
  Pallas kernels: 13.2 us -> 6.83 us
  waiting for transfers between devices: 4.79 us -> 0 us
  starting transfers between devices: 3.35 us -> 0 us
  local copies, waits for them, and re-layouts: 4.21 us -> 2.22 us
    all_gather x8 -> x7, blocking collectives: 50.5 us -> 38.5 us  [on_device(): chip = lax.all_gather(rounded, 'core')]
    all_gather x0 -> x1, blocking collectives: none -> 12 us  [on_device(): chip, hot = spread(lax.all_gather(packed, 'core'), packed, blocks)]
    all_to_all x7 -> x8, blocking collectives: 59.1 us -> 67.5 us  [on_device(): pool = lax.all_to_all(chip, ALL, 0, 0, axis_index_groups=groups)]
    all_to_all x1 -> x0, waiting for transfers between devices: 4.79 us -> none  [on_device(): pool = lax.all_to_all(chip, ALL, 0, 0, axis_index_groups=groups)]
    pallas_call x8 -> x9, Pallas kernels: 10.3 us -> 6.03 us  [the longest x7 5.08 us: step(): pl.pallas_call(functools.partial(step_kernel, k), out_shape=(shape(BR, BL...]
    all_to_all x1 -> x0, starting transfers between devices: 3.35 us -> none  [on_device(): pool = lax.all_to_all(chip, ALL, 0, 0, axis_index_groups=groups)]
    pallas_call x1, Pallas kernels: 2.89 us -> 0.81 us  [on_device(): pl.pallas_call(functools.partial(factor_kernel, DOMS * SUBS * BR * BLK),...]
  transfers between devices with their start and end apart: 1 -> 0, of which waited for: 1 -> 0; matrix products, arithmetic and copies ran while one was open for 1% -> 0% of each run, Pallas kernels for 0% -> 0%
where the time goes in v2:
time: 163 us; the launch traced here: 162 us
  blocking collectives  151 us (93%)
  Pallas kernels  6.83 us (4%)
  local copies, waits for them, and re-layouts  2.22 us (1%)
    all_to_all x8, blocking collectives, on_device(): pool = lax.all_to_all(chip, ALL, 0, 0, axis_index_groups=groups)  67.5 us
    all_gather x7, blocking collectives, on_device(): chip = lax.all_gather(rounded, 'core')  38.5 us
    all_to_all x2, blocking collectives, to_all(): lax.all_to_all(jnp.broadcast_to(value, (peers,) + value.shape), axes, 0, 0)  32.7 us
    all_gather x1, blocking collectives, on_device(): chip, hot = spread(lax.all_gather(packed, 'core'), packed, blocks)  12 us
    pallas_call x7, Pallas kernels, step(): pl.pallas_call(functools.partial(step_kernel, k), out_shape=(shape(BR, BL...  5.08 us

profile of v2, /device:TPU:1, one launch (start us, length us, event | category | flops | bytes accessed | tf_op | source)
XLA Modules:
  0.0 162.0 jit_solution(5689413477284507770)
XLA Ops:
  0.6 0.7 fusion.1
  1.3 0.1 copy.10
  1.4 0.7 select_maximum_fusion.packed_ref.v_ref.refs_0_
  2.1 12.0 %all-gather = f32[80,128]{1,0:T(8,128)S(1)} all-gather(f32[40,128]{1,0:T(8,128)S(1)} %select_maximum_fusion.packed_ref.v_ref.refs_0_), channel_id=2, replica_groups=mesh['y'=8,'z'=12,'core'=2,'sub'=4] {'core'}, dimensions={0}, use_global_device_ids=true | all-gather | bytes 61440 | tf_op jit(solution)/shard_map/all_gather | solution.py:203
  14.1 2.0 %copy-done = bf16[1,1,16,7,128,128]{5,4,3,2,1,0:T(8,128)(2,1)S(1)} copy-done((bf16[1,1,16,7,128,128]{5,4,3,2,1,0:T(8,128)(2,1)S(1)}, bf16[1,1,16,7,128,128]{5,4,3,2,1,0:T(8,128)(2,1)}, u32[]{:S(2)}) %copy-start) | copy-done | bytes 3670040
  16.2 0.1 spread.1
  16.3 8.4 %all_to_all.50.pool_ref = bf16[8,2,16,128]{3,2,1,0:T(8,128)(2,1)S(1)} all-to-all(bf16[8,2,16,128]{3,2,1,0:T(8,128)(2,1)S(1)} %get-tuple-element.22), channel_id=1, replica_groups={{764,765,766,767,0,1,2,3},{4,5,6,7,8,9,10,11},{12,13,14,15,16,17,18,19}..., dimensions={0} | all-to-all | bytes 131072 | tf_op jit(solution)/shard_map/all_to_all | solution.py:207
  24.7 0.7 step.7
  25.4 8.7 %all-gather.1 = bf16[32,128]{1,0:T(8,128)(2,1)S(1)} all-gather(bf16[16,128]{1,0:T(8,128)(2,1)S(1)} %get-tuple-element.24), channel_id=3, replica_groups=mesh['y'=8,'z'=12,'core'=2,'sub'=4] {'core'}, dimensions={0}, use_global_device_ids=true | all-gather | bytes 12288 | tf_op jit(solution)/shard_map/all_gather | solution.py:205
  34.1 8.4 %all_to_all.51.pool_ref = bf16[8,2,16,128]{3,2,1,0:T(8,128)(2,1)S(1)} all-to-all(bf16[8,2,16,128]{3,2,1,0:T(8,128)(2,1)S(1)} %broadcast_in_dim.27), channel_id=1, replica_groups={{764,765,766,767,0,1,2,3},{4,5,6,7,8,9,10,11},{12,13,14,15,16,17,18,19}..., dimensions={0} | all-to-all | bytes 131072 | tf_op jit(solution)/shard_map/all_to_all | solution.py:207
  42.5 0.7 step.8
  43.3 5.0 %all-gather.2 = bf16[32,128]{1,0:T(8,128)(2,1)S(1)} all-gather(bf16[16,128]{1,0:T(8,128)(2,1)S(1)} %get-tuple-element.26), channel_id=4, replica_groups=mesh['y'=8,'z'=12,'core'=2,'sub'=4] {'core'}, dimensions={0}, use_global_device_ids=true | all-gather | bytes 12288 | tf_op jit(solution)/shard_map/all_gather | solution.py:205
  48.3 8.4 %all_to_all.52.pool_ref = bf16[8,2,16,128]{3,2,1,0:T(8,128)(2,1)S(1)} all-to-all(bf16[8,2,16,128]{3,2,1,0:T(8,128)(2,1)S(1)} %broadcast_in_dim.28), channel_id=1, replica_groups={{764,765,766,767,0,1,2,3},{4,5,6,7,8,9,10,11},{12,13,14,15,16,17,18,19}..., dimensions={0} | all-to-all | bytes 131072 | tf_op jit(solution)/shard_map/all_to_all | solution.py:207
  56.7 0.7 step.9
  57.4 5.0 %all-gather.3 = bf16[32,128]{1,0:T(8,128)(2,1)S(1)} all-gather(bf16[16,128]{1,0:T(8,128)(2,1)S(1)} %get-tuple-element.28), channel_id=5, replica_groups=mesh['y'=8,'z'=12,'core'=2,'sub'=4] {'core'}, dimensions={0}, use_global_device_ids=true | all-gather | bytes 12288 | tf_op jit(solution)/shard_map/all_gather | solution.py:205
  62.4 8.4 %all_to_all.53.pool_ref = bf16[8,2,16,128]{3,2,1,0:T(8,128)(2,1)S(1)} all-to-all(bf16[8,2,16,128]{3,2,1,0:T(8,128)(2,1)S(1)} %broadcast_in_dim.29), channel_id=1, replica_groups={{764,765,766,767,0,1,2,3},{4,5,6,7,8,9,10,11},{12,13,14,15,16,17,18,19}..., dimensions={0} | all-to-all | bytes 131072 | tf_op jit(solution)/shard_map/all_to_all | solution.py:207
  70.9 0.7 step.10
  71.6 5.0 %all-gather.4 = bf16[32,128]{1,0:T(8,128)(2,1)S(1)} all-gather(bf16[16,128]{1,0:T(8,128)(2,1)S(1)} %get-tuple-element.30), channel_id=6, replica_groups=mesh['y'=8,'z'=12,'core'=2,'sub'=4] {'core'}, dimensions={0}, use_global_device_ids=true | all-gather | bytes 12288 | tf_op jit(solution)/shard_map/all_gather | solution.py:205
  76.6 8.4 %all_to_all.54.pool_ref = bf16[8,2,16,128]{3,2,1,0:T(8,128)(2,1)S(1)} all-to-all(bf16[8,2,16,128]{3,2,1,0:T(8,128)(2,1)S(1)} %broadcast_in_dim.30), channel_id=1, replica_groups={{764,765,766,767,0,1,2,3},{4,5,6,7,8,9,10,11},{12,13,14,15,16,17,18,19}..., dimensions={0} | all-to-all | bytes 131072 | tf_op jit(solution)/shard_map/all_to_all | solution.py:207
  85.0 0.7 step.11
  85.8 5.0 %all-gather.5 = bf16[32,128]{1,0:T(8,128)(2,1)S(1)} all-gather(bf16[16,128]{1,0:T(8,128)(2,1)S(1)} %get-tuple-element.32), channel_id=7, replica_groups=mesh['y'=8,'z'=12,'core'=2,'sub'=4] {'core'}, dimensions={0}, use_global_device_ids=true | all-gather | bytes 12288 | tf_op jit(solution)/shard_map/all_gather | solution.py:205
  90.8 8.4 %all_to_all.55.pool_ref = bf16[8,2,16,128]{3,2,1,0:T(8,128)(2,1)S(1)} all-to-all(bf16[8,2,16,128]{3,2,1,0:T(8,128)(2,1)S(1)} %broadcast_in_dim.31), channel_id=1, replica_groups={{764,765,766,767,0,1,2,3},{4,5,6,7,8,9,10,11},{12,13,14,15,16,17,18,19}..., dimensions={0} | all-to-all | bytes 131072 | tf_op jit(solution)/shard_map/all_to_all | solution.py:207
  99.2 0.7 step.12
  99.9 5.0 %all-gather.6 = bf16[32,128]{1,0:T(8,128)(2,1)S(1)} all-gather(bf16[16,128]{1,0:T(8,128)(2,1)S(1)} %get-tuple-element.34), channel_id=8, replica_groups=mesh['y'=8,'z'=12,'core'=2,'sub'=4] {'core'}, dimensions={0}, use_global_device_ids=true | all-gather | bytes 12288 | tf_op jit(solution)/shard_map/all_gather | solution.py:205
  104.9 8.4 %all_to_all.56.pool_ref = bf16[8,2,16,128]{3,2,1,0:T(8,128)(2,1)S(1)} all-to-all(bf16[8,2,16,128]{3,2,1,0:T(8,128)(2,1)S(1)} %broadcast_in_dim.32), channel_id=1, replica_groups={{764,765,766,767,0,1,2,3},{4,5,6,7,8,9,10,11},{12,13,14,15,16,17,18,19}..., dimensions={0} | all-to-all | bytes 131072 | tf_op jit(solution)/shard_map/all_to_all | solution.py:207
  113.4 0.7 step.13
  114.1 5.0 %all-gather.7 = bf16[32,128]{1,0:T(8,128)(2,1)S(1)} all-gather(bf16[16,128]{1,0:T(8,128)(2,1)S(1)} %get-tuple-element.36), channel_id=9, replica_groups=mesh['y'=8,'z'=12,'core'=2,'sub'=4] {'core'}, dimensions={0}, use_global_device_ids=true | all-gather | bytes 12288 | tf_op jit(solution)/shard_map/all_gather | solution.py:205
  119.1 8.4 %all_to_all.57.pool_ref = bf16[8,2,16,128]{3,2,1,0:T(8,128)(2,1)S(1)} all-to-all(bf16[8,2,16,128]{3,2,1,0:T(8,128)(2,1)S(1)} %broadcast_in_dim.33), channel_id=1, replica_groups={{764,765,766,767,0,1,2,3},{4,5,6,7,8,9,10,11},{12,13,14,15,16,17,18,19}..., dimensions={0} | all-to-all | bytes 131072 | tf_op jit(solution)/shard_map/all_to_all | solution.py:207
  127.5 0.8 last.1
  128.4 13.9 %all_to_all.58 = f32[32,8,128]{2,1,0:T(8,128)S(1)} all-to-all(f32[32,8,128]{2,1,0:T(8,128)S(1)} %broadcast_in_dim.34), channel_id=1, replica_groups=mesh['y'=8,'z'=12,'core'=2,'sub'=4] {'y','sub'}, dimensions={0} | all-to-all | bytes 262144 | tf_op jit(solution)/shard_map/all_to_all | solution.py:190
  142.3 18.9 %all_to_all.59.parts_ref = f32[24,8,128]{2,1,0:T(8,128)S(1)} all-to-all(f32[24,8,128]{2,1,0:T(8,128)S(1)} %broadcast_in_dim.35), channel_id=1, replica_groups=mesh['y'=8,'z'=12,'core'=2,'sub'=4] {'z','core'}, dimensions={0} | all-to-all | bytes 196608 | tf_op jit(solution)/shard_map/all_to_all | solution.py:190
  161.2 0.8 factor.1
  (13 shorter events, 0.1 us)
Async XLA Ops:
  14.1 2.0 %copy-start = (bf16[1,1,16,7,128,128]{5,4,3,2,1,0:T(8,128)(2,1)S(1)}, bf16[1,1,16,7,128,128]{5,4,3,2,1,0:T(8,128)(2,1)}, u32[]{:S(2)}) copy-start(bf16[1,1,16,7,128,128]{5,4,3,2,1,0:T(8,128)(2,1)} %param.5) | copy-start | bytes 11010052
  16.2 8.5 %copy-start.1 = (bf16[1,1,16,7,128,128]{5,4,3,2,1,0:T(8,128)(2,1)S(1)}, bf16[1,1,16,7,128,128]{5,4,3,2,1,0:T(8,128)(2,1)}, u32[]{:S(2)}) copy-start(bf16[1,1,16,7,128,128]{5,4,3,2,1,0:T(8,128)(2,1)} %param.5) | copy-start | bytes 11010052

commit v3 on v2

--- a/solution.py
+++ b/solution.py
@@ -17,6 +17,7 @@
 NY, NZ, NCORE = 8, 12, 2
 DOMS = NY * NZ * NCORE
 CHIPS = DOMS // NCORE
+GAP = 16
 PEERS = 2 * SUBS
 POOL = PEERS * NCORE * BR
 DOM = ("y", "z", "core")
@@ -45,15 +46,18 @@
     return jnp.where(inside, index, -1)
 
 
-def one_hot(columns):
-    rows = pool_rows(columns)
+def one_hot(lines):
     place = lax.broadcasted_iota(jnp.int32, (BR, POOL), 1)
-    return jnp.concatenate(
-        [jnp.where(rows[:, n:n + 1] == place, 1.0, 0.0) for n in range(NB)], axis=0
-    ).astype(jnp.bfloat16)
-
-
-def product(k, pool_ref, hot_ref, blocks_ref, v_ref, packed_ref):
+    own = lax.broadcasted_iota(jnp.int32, (BR, BLK), 0) == lax.broadcasted_iota(jnp.int32, (BR, BLK), 1)
+    parts = []
+    for line in lines:
+        rows = pool_rows(line).astype(jnp.float32)
+        down = jnp.sum(jnp.where(own, rows, 0.0), axis=1, keepdims=True).astype(jnp.int32)
+        parts.append(jnp.where(down == place, 1.0, 0.0))
+    return jnp.concatenate(parts, axis=0).astype(jnp.bfloat16)
+
+
+def product(k, pool_ref, hot_ref, blocks_ref, v_ref, shifts_ref):
     pool = pool_ref[...].reshape(POOL, BLK)
     picked = jnp.dot(hot_ref[...], pool, preferred_element_type=jnp.float32)
     fields = [picked[n * BR:(n + 1) * BR] for n in range(NB)]
@@ -82,18 +86,24 @@
         if singles:
             by_vector = vector_unit(singles.pop(0), by_vector)
     image = jnp.where(row < MATRIX_ROWS, by_matrix, by_vector.T[:BR])
-    return image - packed_ref[2 * BR:2 * BR + 1, k:k + 1] * v_ref[0:BR, :]
-
-
-def spread_kernel(both_ref, packed_ref, blocks_ref, out_ref, hot_ref):
-    both = both_ref[:, 0:BR, :].astype(jnp.bfloat16)
+    return image - shifts_ref[0:1, k:k + 1] * v_ref[0:BR, :]
+
+
+def spread_kernel(both_ref, *refs):
+    out_ref = refs[-1]
+    both = both_ref[...].astype(jnp.bfloat16)
     for i in range(PEERS):
         out_ref[i] = both
-    hot_ref[...] = one_hot(packed_ref[BR:2 * BR, :].astype(jnp.int32))
-
-
-def step_kernel(k, pool_ref, hot_ref, blocks_ref, v_ref, packed_ref, out_ref, rounded_ref):
-    new = product(k, pool_ref, hot_ref, blocks_ref, v_ref, packed_ref)
+
+
+def first_kernel(pool_ref, columns_ref, blocks_ref, v_ref, shifts_ref, out_ref, rounded_ref, hot_ref):
+    wide = jnp.zeros((1, BLK - BR), jnp.int32)
+    hot_ref[...] = one_hot([jnp.concatenate([columns_ref[n], wide], axis=1) for n in range(NB)])
+    step_kernel(0, pool_ref, hot_ref, blocks_ref, v_ref, shifts_ref, out_ref, rounded_ref)
+
+
+def step_kernel(k, pool_ref, hot_ref, blocks_ref, v_ref, shifts_ref, out_ref, rounded_ref):
+    new = product(k, pool_ref, hot_ref, blocks_ref, v_ref, shifts_ref)
     out_ref[...] = new
     rounded_ref[...] = new.astype(jnp.bfloat16)
 
@@ -106,26 +116,33 @@
     return jnp.sum(stack, axis=1, keepdims=True)
 
 
-def last_kernel(pool_ref, hot_ref, blocks_ref, packed_ref, *refs):
+def last_kernel(pool_ref, hot_ref, blocks_ref, shifts_ref, *refs):
     ins, out_ref, gram_ref = refs[:S], refs[S], refs[S + 1]
-    new = product(S - 1, pool_ref, hot_ref, blocks_ref, ins[-1], packed_ref)
+    new = product(S - 1, pool_ref, hot_ref, blocks_ref, ins[-1], shifts_ref)
     out_ref[...] = new
     vectors = [ref[0:BR, :] for ref in ins] + [new]
-    lane = lax.broadcasted_iota(jnp.int32, (S, BLK), 1)
+    lane = lax.broadcasted_iota(jnp.int32, (S, BLK), 1) - GAP * lax.broadcasted_iota(jnp.int32, (S, BLK), 0)
     tile = jnp.zeros((S, BLK), jnp.float32)
     for i in range(S1):
-        tile = jnp.where(lane == i, inner(vectors[i], vectors[:min(i + 1, S)]), tile)
-    gram_ref[...] = jnp.where(lane == S1, inner(new, [new]), tile)
+        count = min(i + 1, S)
+        tile = jnp.where((lane == i), inner(vectors[i], vectors[:count]), tile)
+    row = jnp.sum(tile, axis=0, keepdims=True)
+    place = lax.broadcasted_iota(jnp.int32, (1, BLK), 1)
+    corner = jnp.sum(jnp.sum(new * new, axis=0, keepdims=True), axis=1, keepdims=True)
+    gram_ref[...] = jnp.where(place == S1, corner, row)
 
 
 def factor_kernel(rows_total, parts_ref, *refs):
     out_ref, basis_ref = refs[S1], refs[S1 + 1]
     for i in range(S1):
         basis_ref[i] = refs[i][0:BR, :]
-    tile = jnp.sum(parts_ref[...], axis=0) / rows_total
-    spread = [jnp.broadcast_to(tile[:, i:i + 1], (S, BLK)) for i in range(S1 + 1)]
-    a = {(j, i): jnp.broadcast_to(spread[i][j:j + 1], (S, BLK)) for i in range(S1) for j in range(min(i + 1, S))}
-    a[S, S] = jnp.broadcast_to(spread[S1][0:1], (S, BLK))
+    tile = jnp.broadcast_to(jnp.sum(parts_ref[...], axis=0) / rows_total, (S, BLK))
+
+    def spread_lane(p):
+        return jnp.broadcast_to(tile[:, p:p + 1], (S, BLK))
+
+    a = {(j, i): spread_lane(GAP * j + i) for i in range(S1) for j in range(min(i + 1, S))}
+    a[S, S] = spread_lane(S1)
     sub = lax.broadcasted_iota(jnp.int32, (S, BLK), 0)
     lane = lax.broadcasted_iota(jnp.int32, (S, BLK), 1)
     top = jnp.zeros((S, BLK), jnp.float32)
@@ -150,21 +167,33 @@
     return jax.ShapeDtypeStruct(dims, dtype)
 
 
-def spread(both, packed, blocks):
+def spread(both, *others):
     return pl.pallas_call(
         spread_kernel,
+        out_shape=shape(PEERS, NCORE, BR, BLK, dtype=jnp.bfloat16),
+        in_specs=[VMEM] + [pl.BlockSpec(memory_space=pl.ANY)] * len(others),
+        out_specs=VMEM,
+        compiler_params=pltpu.CompilerParams(vmem_limit_bytes=58 * 1024 * 1024),
+        name="spread",
+    )(both, *others)
+
+
+def first_step(pool, columns, blocks, v, shifts):
+    return pl.pallas_call(
+        first_kernel,
         out_shape=(
-            shape(PEERS, NCORE, BR, BLK, dtype=jnp.bfloat16),
+            shape(BR, BLK),
+            shape(BR, BLK, dtype=jnp.bfloat16),
             shape(NB * BR, POOL, dtype=jnp.bfloat16),
         ),
-        in_specs=[VMEM] * 3,
-        out_specs=(VMEM,) * 2,
-        compiler_params=PARAMS,
-        name="spread",
-    )(both, packed, blocks)
-
-
-def step(k, pool, hot, blocks, v, packed):
+        in_specs=[VMEM] * 5,
+        out_specs=(VMEM,) * 3,
+        compiler_params=PARAMS,
+        name="first",
+    )(pool, columns, blocks, v, shifts)
+
+
+def step(k, pool, hot, blocks, v, shifts):
     return pl.pallas_call(
         functools.partial(step_kernel, k),
         out_shape=(shape(BR, BLK), shape(BR, BLK, dtype=jnp.bfloat16)),
@@ -172,18 +201,18 @@
         out_specs=(VMEM, VMEM),
         compiler_params=PARAMS,
         name="step",
-    )(pool, hot, blocks, v, packed)
-
-
-def last_step(pool, hot, blocks, packed, vectors):
+    )(pool, hot, blocks, v, shifts)
+
+
+def last_step(pool, hot, blocks, shifts, vectors):
     return pl.pallas_call(
         last_kernel,
-        out_shape=(shape(BR, BLK), shape(S, BLK)),
+        out_shape=(shape(BR, BLK), shape(1, BLK)),
         in_specs=[VMEM] * (4 + S),
         out_specs=(VMEM, VMEM),
         compiler_params=PARAMS,
         name="last",
-    )(pool, hot, blocks, packed, *vectors)
+    )(pool, hot, blocks, shifts, *vectors)
 
 
 def to_all(value, axes, peers):
@@ -192,23 +221,23 @@
 
 def on_device(groups, start_vector, blocks, columns, shifts):
     blocks = blocks[0, 0]
-    packed = jnp.concatenate([
-        start_vector[0, 0],
-        jnp.pad(columns[0, 0].astype(jnp.float32), ((0, 0), (0, BLK - NB))),
-        jnp.pad(shifts.reshape(1, S), ((0, 7), (0, BLK - S))),
-    ], axis=0)
-    vectors = [packed]
+    columns = columns[0].transpose(2, 0, 1)
+    shifts = shifts.reshape(1, S)
+    v = start_vector[0, 0]
+    vectors = [v]
+    chip = spread(lax.all_gather(v, "core"), v, blocks, columns, shifts)
     for k in range(S):
-        if k == 0:
-            chip, hot = spread(lax.all_gather(packed, "core"), packed, blocks)
-        else:
+        if k > 0:
             chip = lax.all_gather(rounded, "core")
             chip = jnp.broadcast_to(chip, (PEERS,) + chip.shape)
         pool = lax.all_to_all(chip, ALL, 0, 0, axis_index_groups=groups)
+        if k == 0:
+            v, rounded, hot = first_step(pool, columns, blocks, v, shifts)
+        elif k < S - 1:
+            v, rounded = step(k, pool, hot, blocks, v, shifts)
         if k < S - 1:
-            v, rounded = step(k, pool, hot, blocks, vectors[-1], packed)
             vectors.append(v)
-    v, gram = last_step(pool, hot, blocks, packed, vectors)
+    v, gram = last_step(pool, hot, blocks, shifts, vectors)
     gram = jnp.sum(to_all(gram, ("y", "sub"), NY * SUBS), axis=0)
     parts = to_all(gram, ("z", "core"), NZ * NCORE)
     factor, basis = pl.pallas_call(

time: 163 us -> 160 us (0.982)
  local copies, waits for them, and re-layouts: 2.22 us -> 0.12 us
    all_to_all x2, blocking collectives: 32.7 us -> 30.4 us  [to_all(): lax.all_to_all(jnp.broadcast_to(value, (peers,) + value.shape), axes, 0, 0)]
    pallas_call x2 -> x3, Pallas kernels: 0.94 us -> 3.02 us  [the longest x1 1.35 us: spread(): pl.pallas_call(spread_kernel, out_shape=shape(PEERS, NCORE, BR, BLK, dtyp...]
    unnamed x4 -> x8, local copies, waits for them, and re-layouts: 2.04 us -> 0.03 us
    all_gather x1, blocking collectives: 12 us -> 13.9 us  [on_device(): chip = spread(lax.all_gather(v, 'core'), v, blocks, columns, shifts)]
    pallas_call x7 -> x6, Pallas kernels: 5.08 us -> 4.27 us  [step(): pl.pallas_call(functools.partial(step_kernel, k), out_shape=(shape(BR, BL...]
where the time goes in v3:
time: 160 us; the launch traced here: 159 us
  blocking collectives  151 us (94%)
  Pallas kernels  8.11 us (5%)
    all_to_all x8, blocking collectives, on_device(): pool = lax.all_to_all(chip, ALL, 0, 0, axis_index_groups=groups)  68.2 us
    all_gather x7, blocking collectives, on_device(): chip = lax.all_gather(rounded, 'core')  38.1 us
    all_to_all x2, blocking collectives, to_all(): lax.all_to_all(jnp.broadcast_to(value, (peers,) + value.shape), axes, 0, 0)  30.4 us
    all_gather x1, blocking collectives, on_device(): chip = spread(lax.all_gather(v, 'core'), v, blocks, columns, shifts)  13.9 us
    pallas_call x6, Pallas kernels, step(): pl.pallas_call(functools.partial(step_kernel, k), out_shape=(shape(BR, BL...  4.27 us

profile of v3, /device:TPU:1, one launch (start us, length us, event | category | flops | bytes accessed | tf_op | source)
XLA Modules:
  0.0 159.5 jit_solution(1865784298115681309)
XLA Ops:
  0.6 0.0 copy-start.1
  0.6 0.0 copy-start.2
  0.7 0.0 copy-start.3
  0.7 0.0 copy-start
  0.7 13.9 %all-gather = f32[2,1,16,128]{3,2,1,0:T(8,128)} all-gather(f32[1,1,16,128]{3,2,1,0:T(8,128)} %param.4), channel_id=2, replica_groups=mesh['y'=8,'z'=12,'core'=2,'sub'=4] {'core'}, dimensions={0}, use_global_device_ids=true | all-gather | bytes 24576 | tf_op jit(solution)/shard_map/all_gather | solution.py:228
  14.6 1.4 spread.1
  15.9 9.0 %all_to_all.50.pool_ref = bf16[8,2,16,128]{3,2,1,0:T(8,128)(2,1)S(1)} all-to-all(bf16[8,2,16,128]{3,2,1,0:T(8,128)(2,1)} %spread.1), channel_id=1, replica_groups={{764,765,766,767,0,1,2,3},{4,5,6,7,8,9,10,11},{12,13,14,15,16,17,18,19}..., dimensions={0} | all-to-all | bytes 131072 | tf_op jit(solution)/shard_map/all_to_all | solution.py:233
  25.0 0.8 first.1
  25.8 8.0 %all-gather.1 = bf16[32,128]{1,0:T(8,128)(2,1)S(1)} all-gather(bf16[16,128]{1,0:T(8,128)(2,1)S(1)} %get-tuple-element.21), channel_id=3, replica_groups=mesh['y'=8,'z'=12,'core'=2,'sub'=4] {'core'}, dimensions={0}, use_global_device_ids=true | all-gather | bytes 12288 | tf_op jit(solution)/shard_map/all_gather | solution.py:231
  33.8 8.4 %all_to_all.51.pool_ref = bf16[8,2,16,128]{3,2,1,0:T(8,128)(2,1)S(1)} all-to-all(bf16[8,2,16,128]{3,2,1,0:T(8,128)(2,1)S(1)} %broadcast_in_dim.27), channel_id=1, replica_groups={{764,765,766,767,0,1,2,3},{4,5,6,7,8,9,10,11},{12,13,14,15,16,17,18,19}..., dimensions={0} | all-to-all | bytes 131072 | tf_op jit(solution)/shard_map/all_to_all | solution.py:233
  42.3 0.7 step.6
  43.0 5.0 %all-gather.2 = bf16[32,128]{1,0:T(8,128)(2,1)S(1)} all-gather(bf16[16,128]{1,0:T(8,128)(2,1)S(1)} %get-tuple-element.24), channel_id=4, replica_groups=mesh['y'=8,'z'=12,'core'=2,'sub'=4] {'core'}, dimensions={0}, use_global_device_ids=true | all-gather | bytes 12288 | tf_op jit(solution)/shard_map/all_gather | solution.py:231
  48.0 8.4 %all_to_all.52.pool_ref = bf16[8,2,16,128]{3,2,1,0:T(8,128)(2,1)S(1)} all-to-all(bf16[8,2,16,128]{3,2,1,0:T(8,128)(2,1)S(1)} %broadcast_in_dim.28), channel_id=1, replica_groups={{764,765,766,767,0,1,2,3},{4,5,6,7,8,9,10,11},{12,13,14,15,16,17,18,19}..., dimensions={0} | all-to-all | bytes 131072 | tf_op jit(solution)/shard_map/all_to_all | solution.py:233
  56.4 0.7 step.7
  57.2 5.0 %all-gather.3 = bf16[32,128]{1,0:T(8,128)(2,1)S(1)} all-gather(bf16[16,128]{1,0:T(8,128)(2,1)S(1)} %get-tuple-element.26), channel_id=5, replica_groups=mesh['y'=8,'z'=12,'core'=2,'sub'=4] {'core'}, dimensions={0}, use_global_device_ids=true | all-gather | bytes 12288 | tf_op jit(solution)/shard_map/all_gather | solution.py:231
  62.2 8.4 %all_to_all.53.pool_ref = bf16[8,2,16,128]{3,2,1,0:T(8,128)(2,1)S(1)} all-to-all(bf16[8,2,16,128]{3,2,1,0:T(8,128)(2,1)S(1)} %broadcast_in_dim.29), channel_id=1, replica_groups={{764,765,766,767,0,1,2,3},{4,5,6,7,8,9,10,11},{12,13,14,15,16,17,18,19}..., dimensions={0} | all-to-all | bytes 131072 | tf_op jit(solution)/shard_map/all_to_all | solution.py:233
  70.6 0.7 step.8
  71.3 5.0 %all-gather.4 = bf16[32,128]{1,0:T(8,128)(2,1)S(1)} all-gather(bf16[16,128]{1,0:T(8,128)(2,1)S(1)} %get-tuple-element.28), channel_id=6, replica_groups=mesh['y'=8,'z'=12,'core'=2,'sub'=4] {'core'}, dimensions={0}, use_global_device_ids=true | all-gather | bytes 12288 | tf_op jit(solution)/shard_map/all_gather | solution.py:231
  76.4 8.4 %all_to_all.54.pool_ref = bf16[8,2,16,128]{3,2,1,0:T(8,128)(2,1)S(1)} all-to-all(bf16[8,2,16,128]{3,2,1,0:T(8,128)(2,1)S(1)} %broadcast_in_dim.30), channel_id=1, replica_groups={{764,765,766,767,0,1,2,3},{4,5,6,7,8,9,10,11},{12,13,14,15,16,17,18,19}..., dimensions={0} | all-to-all | bytes 131072 | tf_op jit(solution)/shard_map/all_to_all | solution.py:233
  84.8 0.7 step.9
  85.5 5.0 %all-gather.5 = bf16[32,128]{1,0:T(8,128)(2,1)S(1)} all-gather(bf16[16,128]{1,0:T(8,128)(2,1)S(1)} %get-tuple-element.30), channel_id=7, replica_groups=mesh['y'=8,'z'=12,'core'=2,'sub'=4] {'core'}, dimensions={0}, use_global_device_ids=true | all-gather | bytes 12288 | tf_op jit(solution)/shard_map/all_gather | solution.py:231
  90.5 8.4 %all_to_all.55.pool_ref = bf16[8,2,16,128]{3,2,1,0:T(8,128)(2,1)S(1)} all-to-all(bf16[8,2,16,128]{3,2,1,0:T(8,128)(2,1)S(1)} %broadcast_in_dim.31), channel_id=1, replica_groups={{764,765,766,767,0,1,2,3},{4,5,6,7,8,9,10,11},{12,13,14,15,16,17,18,19}..., dimensions={0} | all-to-all | bytes 131072 | tf_op jit(solution)/shard_map/all_to_all | solution.py:233
  99.0 0.7 step.10
  99.7 5.0 %all-gather.6 = bf16[32,128]{1,0:T(8,128)(2,1)S(1)} all-gather(bf16[16,128]{1,0:T(8,128)(2,1)S(1)} %get-tuple-element.32), channel_id=8, replica_groups=mesh['y'=8,'z'=12,'core'=2,'sub'=4] {'core'}, dimensions={0}, use_global_device_ids=true | all-gather | bytes 12288 | tf_op jit(solution)/shard_map/all_gather | solution.py:231
  104.7 8.4 %all_to_all.56.pool_ref = bf16[8,2,16,128]{3,2,1,0:T(8,128)(2,1)S(1)} all-to-all(bf16[8,2,16,128]{3,2,1,0:T(8,128)(2,1)S(1)} %broadcast_in_dim.32), channel_id=1, replica_groups={{764,765,766,767,0,1,2,3},{4,5,6,7,8,9,10,11},{12,13,14,15,16,17,18,19}..., dimensions={0} | all-to-all | bytes 131072 | tf_op jit(solution)/shard_map/all_to_all | solution.py:233
  113.2 0.7 step.11
  113.9 5.0 %all-gather.7 = bf16[32,128]{1,0:T(8,128)(2,1)S(1)} all-gather(bf16[16,128]{1,0:T(8,128)(2,1)S(1)} %get-tuple-element.34), channel_id=9, replica_groups=mesh['y'=8,'z'=12,'core'=2,'sub'=4] {'core'}, dimensions={0}, use_global_device_ids=true | all-gather | bytes 12288 | tf_op jit(solution)/shard_map/all_gather | solution.py:231
  118.9 8.4 %all_to_all.57.pool_ref = bf16[8,2,16,128]{3,2,1,0:T(8,128)(2,1)S(1)} all-to-all(bf16[8,2,16,128]{3,2,1,0:T(8,128)(2,1)S(1)} %broadcast_in_dim.33), channel_id=1, replica_groups={{764,765,766,767,0,1,2,3},{4,5,6,7,8,9,10,11},{12,13,14,15,16,17,18,19}..., dimensions={0} | all-to-all | bytes 131072 | tf_op jit(solution)/shard_map/all_to_all | solution.py:233
  127.4 0.9 last.1
  128.3 13.1 %all_to_all.58 = f32[32,1,128]{2,1,0:T(1,128)S(1)} all-to-all(f32[32,1,128]{2,1,0:T(1,128)S(1)} %broadcast_in_dim.34), channel_id=1, replica_groups=mesh['y'=8,'z'=12,'core'=2,'sub'=4] {'y','sub'}, dimensions={0} | all-to-all | bytes 32768 | tf_op jit(solution)/shard_map/all_to_all | solution.py:219
  141.4 17.3 %all_to_all.59.parts_ref = f32[24,1,128]{2,1,0:T(1,128)S(1)} all-to-all(f32[24,1,128]{2,1,0:T(1,128)S(1)} %broadcast_in_dim.35), channel_id=1, replica_groups=mesh['y'=8,'z'=12,'core'=2,'sub'=4] {'z','core'}, dimensions={0} | all-to-all | bytes 24576 | tf_op jit(solution)/shard_map/all_to_all | solution.py:219
  158.7 0.8 factor.1
  (14 shorter events, 0.1 us)
Async XLA Ops:
  0.6 24.3 %copy-start.1 = (f32[1,1,16,128]{3,2,1,0:T(8,128)S(1)}, f32[1,1,16,128]{3,2,1,0:T(8,128)}, u32[]{:S(2)}) copy-start(f32[1,1,16,128]{3,2,1,0:T(8,128)} %param.4) | copy-start | bytes 24580
  0.6 24.3 %copy-start.2 = (f32[8]{0:T(128)S(1)}, f32[8]{0:T(128)}, u32[]{:S(2)}) copy-start(f32[8]{0:T(128)} %param.7) | copy-start | bytes 100
  0.7 24.3 %copy-start.3 = (s32[1,1,16,7]{2,1,3,0:T(1,128)S(1)}, s32[1,1,16,7]{2,1,3,0:T(1,128)}, u32[]{:S(2)}) copy-start(s32[1,1,16,7]{2,1,3,0:T(1,128)} %param.6) | copy-start | bytes 1348
  0.7 24.3 %copy-start = (bf16[1,1,16,7,128,128]{5,4,3,2,1,0:T(8,128)(2,1)S(1)}, bf16[1,1,16,7,128,128]{5,4,3,2,1,0:T(8,128)(2,1)}, u32[]{:S(2)}) copy-start(bf16[1,1,16,7,128,128]{5,4,3,2,1,0:T(8,128)(2,1)} %param.5) | copy-start | bytes 11010052

commit v4 on v3

--- a/solution.py
+++ b/solution.py
@@ -89,8 +89,11 @@
     return image - shifts_ref[0:1, k:k + 1] * v_ref[0:BR, :]
 
 
-def spread_kernel(both_ref, *refs):
-    out_ref = refs[-1]
+def touch_kernel(*refs):
+    refs[-1][...] = jnp.zeros((S, BLK), jnp.float32)
+
+
+def spread_kernel(both_ref, _, out_ref):
     both = both_ref[...].astype(jnp.bfloat16)
     for i in range(PEERS):
         out_ref[i] = both
@@ -167,15 +170,26 @@
     return jax.ShapeDtypeStruct(dims, dtype)
 
 
-def spread(both, *others):
+def touch(*arrays):
+    return pl.pallas_call(
+        touch_kernel,
+        out_shape=shape(S, BLK),
+        in_specs=[pl.BlockSpec(memory_space=pl.ANY)] * len(arrays),
+        out_specs=VMEM,
+        compiler_params=pltpu.CompilerParams(vmem_limit_bytes=58 * 1024 * 1024),
+        name="touch",
+    )(*arrays)
+
+
+def spread(both, token):
     return pl.pallas_call(
         spread_kernel,
         out_shape=shape(PEERS, NCORE, BR, BLK, dtype=jnp.bfloat16),
-        in_specs=[VMEM] + [pl.BlockSpec(memory_space=pl.ANY)] * len(others),
+        in_specs=[VMEM, pl.BlockSpec(memory_space=pl.ANY)],
         out_specs=VMEM,
-        compiler_params=pltpu.CompilerParams(vmem_limit_bytes=58 * 1024 * 1024),
+        compiler_params=PARAMS,
         name="spread",
-    )(both, *others)
+    )(both, token)
 
 
 def first_step(pool, columns, blocks, v, shifts):
@@ -225,7 +239,8 @@
     shifts = shifts.reshape(1, S)
     v = start_vector[0, 0]
     vectors = [v]
-    chip = spread(lax.all_gather(v, "core"), v, blocks, columns, shifts)
+    both = lax.all_gather(v, "core")
+    chip = spread(both, touch(v, blocks, columns, shifts))
     for k in range(S):
         if k > 0:
             chip = lax.all_gather(rounded, "core")

time: 160 us -> 158 us (0.988)
  blocking collectives: 151 us -> 149 us
where the time goes in v4:
time: 158 us
  blocking collectives  149 us (94%)
  Pallas kernels  7.35 us (5%)
    all_to_all x8, blocking collectives, on_device(): pool = lax.all_to_all(chip, ALL, 0, 0, axis_index_groups=groups)  67.3 us
    all_gather x7, blocking collectives, on_device(): chip = lax.all_gather(rounded, 'core')  38.8 us
    all_to_all x2, blocking collectives, to_all(): lax.all_to_all(jnp.broadcast_to(value, (peers,) + value.shape), axes, 0, 0)  30.4 us
    all_gather x1, blocking collectives, on_device(): both = lax.all_gather(v, 'core')  12.4 us
    pallas_call x6, Pallas kernels, step(): pl.pallas_call(functools.partial(step_kernel, k), out_shape=(shape(BR, BL...  4.27 us

profile of v4, /device:TPU:1, one launch (start us, length us, event | category | flops | bytes accessed | tf_op | source)
XLA Modules:
  0.0 157.6 jit_solution(7117256908574976961)
XLA Ops:
  0.6 0.0 copy-start.1
  0.6 0.0 copy-start.2
  0.7 0.0 copy-start.4
  0.7 12.4 %all-gather = f32[2,1,16,128]{3,2,1,0:T(8,128)S(1)} all-gather(f32[1,1,16,128]{3,2,1,0:T(8,128)} %param.4), channel_id=2, replica_groups=mesh['y'=8,'z'=12,'core'=2,'sub'=4] {'core'}, dimensions={0}, use_global_device_ids=true | all-gather | bytes 24576 | tf_op jit(solution)/shard_map/all_gather | solution.py:242
  13.0 0.6 touch.1._
  13.6 0.7 copy-done.3
  14.3 8.1 %all_to_all.50.pool_ref = bf16[8,2,16,128]{3,2,1,0:T(8,128)(2,1)S(1)} all-to-all(bf16[8,2,16,128]{3,2,1,0:T(8,128)(2,1)S(1)} %spread.1), channel_id=1, replica_groups={{764,765,766,767,0,1,2,3},{4,5,6,7,8,9,10,11},{12,13,14,15,16,17,18,19}..., dimensions={0} | all-to-all | bytes 131072 | tf_op jit(solution)/shard_map/all_to_all | solution.py:248
  22.5 0.8 first.1
  23.3 8.7 %all-gather.1 = bf16[32,128]{1,0:T(8,128)(2,1)S(1)} all-gather(bf16[16,128]{1,0:T(8,128)(2,1)S(1)} %get-tuple-element.21), channel_id=3, replica_groups=mesh['y'=8,'z'=12,'core'=2,'sub'=4] {'core'}, dimensions={0}, use_global_device_ids=true | all-gather | bytes 12288 | tf_op jit(solution)/shard_map/all_gather | solution.py:246
  32.0 8.4 %all_to_all.51.pool_ref = bf16[8,2,16,128]{3,2,1,0:T(8,128)(2,1)S(1)} all-to-all(bf16[8,2,16,128]{3,2,1,0:T(8,128)(2,1)S(1)} %broadcast_in_dim.27), channel_id=1, replica_groups={{764,765,766,767,0,1,2,3},{4,5,6,7,8,9,10,11},{12,13,14,15,16,17,18,19}..., dimensions={0} | all-to-all | bytes 131072 | tf_op jit(solution)/shard_map/all_to_all | solution.py:248
  40.4 0.7 step.6
  41.1 5.0 %all-gather.2 = bf16[32,128]{1,0:T(8,128)(2,1)S(1)} all-gather(bf16[16,128]{1,0:T(8,128)(2,1)S(1)} %get-tuple-element.24), channel_id=4, replica_groups=mesh['y'=8,'z'=12,'core'=2,'sub'=4] {'core'}, dimensions={0}, use_global_device_ids=true | all-gather | bytes 12288 | tf_op jit(solution)/shard_map/all_gather | solution.py:246
  46.2 8.4 %all_to_all.52.pool_ref = bf16[8,2,16,128]{3,2,1,0:T(8,128)(2,1)S(1)} all-to-all(bf16[8,2,16,128]{3,2,1,0:T(8,128)(2,1)S(1)} %broadcast_in_dim.28), channel_id=1, replica_groups={{764,765,766,767,0,1,2,3},{4,5,6,7,8,9,10,11},{12,13,14,15,16,17,18,19}..., dimensions={0} | all-to-all | bytes 131072 | tf_op jit(solution)/shard_map/all_to_all | solution.py:248
  54.6 0.7 step.7
  55.3 5.0 %all-gather.3 = bf16[32,128]{1,0:T(8,128)(2,1)S(1)} all-gather(bf16[16,128]{1,0:T(8,128)(2,1)S(1)} %get-tuple-element.26), channel_id=5, replica_groups=mesh['y'=8,'z'=12,'core'=2,'sub'=4] {'core'}, dimensions={0}, use_global_device_ids=true | all-gather | bytes 12288 | tf_op jit(solution)/shard_map/all_gather | solution.py:246
  60.3 8.4 %all_to_all.53.pool_ref = bf16[8,2,16,128]{3,2,1,0:T(8,128)(2,1)S(1)} all-to-all(bf16[8,2,16,128]{3,2,1,0:T(8,128)(2,1)S(1)} %broadcast_in_dim.29), channel_id=1, replica_groups={{764,765,766,767,0,1,2,3},{4,5,6,7,8,9,10,11},{12,13,14,15,16,17,18,19}..., dimensions={0} | all-to-all | bytes 131072 | tf_op jit(solution)/shard_map/all_to_all | solution.py:248
  68.8 0.7 step.8
  69.5 5.0 %all-gather.4 = bf16[32,128]{1,0:T(8,128)(2,1)S(1)} all-gather(bf16[16,128]{1,0:T(8,128)(2,1)S(1)} %get-tuple-element.28), channel_id=6, replica_groups=mesh['y'=8,'z'=12,'core'=2,'sub'=4] {'core'}, dimensions={0}, use_global_device_ids=true | all-gather | bytes 12288 | tf_op jit(solution)/shard_map/all_gather | solution.py:246
  74.5 8.4 %all_to_all.54.pool_ref = bf16[8,2,16,128]{3,2,1,0:T(8,128)(2,1)S(1)} all-to-all(bf16[8,2,16,128]{3,2,1,0:T(8,128)(2,1)S(1)} %broadcast_in_dim.30), channel_id=1, replica_groups={{764,765,766,767,0,1,2,3},{4,5,6,7,8,9,10,11},{12,13,14,15,16,17,18,19}..., dimensions={0} | all-to-all | bytes 131072 | tf_op jit(solution)/shard_map/all_to_all | solution.py:248
  83.0 0.7 step.9
  83.7 5.0 %all-gather.5 = bf16[32,128]{1,0:T(8,128)(2,1)S(1)} all-gather(bf16[16,128]{1,0:T(8,128)(2,1)S(1)} %get-tuple-element.30), channel_id=7, replica_groups=mesh['y'=8,'z'=12,'core'=2,'sub'=4] {'core'}, dimensions={0}, use_global_device_ids=true | all-gather | bytes 12288 | tf_op jit(solution)/shard_map/all_gather | solution.py:246
  88.7 8.4 %all_to_all.55.pool_ref = bf16[8,2,16,128]{3,2,1,0:T(8,128)(2,1)S(1)} all-to-all(bf16[8,2,16,128]{3,2,1,0:T(8,128)(2,1)S(1)} %broadcast_in_dim.31), channel_id=1, replica_groups={{764,765,766,767,0,1,2,3},{4,5,6,7,8,9,10,11},{12,13,14,15,16,17,18,19}..., dimensions={0} | all-to-all | bytes 131072 | tf_op jit(solution)/shard_map/all_to_all | solution.py:248
  97.2 0.7 step.10
  97.9 5.0 %all-gather.6 = bf16[32,128]{1,0:T(8,128)(2,1)S(1)} all-gather(bf16[16,128]{1,0:T(8,128)(2,1)S(1)} %get-tuple-element.32), channel_id=8, replica_groups=mesh['y'=8,'z'=12,'core'=2,'sub'=4] {'core'}, dimensions={0}, use_global_device_ids=true | all-gather | bytes 12288 | tf_op jit(solution)/shard_map/all_gather | solution.py:246
  102.9 8.4 %all_to_all.56.pool_ref = bf16[8,2,16,128]{3,2,1,0:T(8,128)(2,1)S(1)} all-to-all(bf16[8,2,16,128]{3,2,1,0:T(8,128)(2,1)S(1)} %broadcast_in_dim.32), channel_id=1, replica_groups={{764,765,766,767,0,1,2,3},{4,5,6,7,8,9,10,11},{12,13,14,15,16,17,18,19}..., dimensions={0} | all-to-all | bytes 131072 | tf_op jit(solution)/shard_map/all_to_all | solution.py:248
  111.4 0.7 step.11
  112.1 5.0 %all-gather.7 = bf16[32,128]{1,0:T(8,128)(2,1)S(1)} all-gather(bf16[16,128]{1,0:T(8,128)(2,1)S(1)} %get-tuple-element.34), channel_id=9, replica_groups=mesh['y'=8,'z'=12,'core'=2,'sub'=4] {'core'}, dimensions={0}, use_global_device_ids=true | all-gather | bytes 12288 | tf_op jit(solution)/shard_map/all_gather | solution.py:246
  117.1 8.4 %all_to_all.57.pool_ref = bf16[8,2,16,128]{3,2,1,0:T(8,128)(2,1)S(1)} all-to-all(bf16[8,2,16,128]{3,2,1,0:T(8,128)(2,1)S(1)} %broadcast_in_dim.33), channel_id=1, replica_groups={{764,765,766,767,0,1,2,3},{4,5,6,7,8,9,10,11},{12,13,14,15,16,17,18,19}..., dimensions={0} | all-to-all | bytes 131072 | tf_op jit(solution)/shard_map/all_to_all | solution.py:248
  125.5 0.9 last.1
  126.4 13.1 %all_to_all.58 = f32[32,1,128]{2,1,0:T(1,128)S(1)} all-to-all(f32[32,1,128]{2,1,0:T(1,128)S(1)} %broadcast_in_dim.34), channel_id=1, replica_groups=mesh['y'=8,'z'=12,'core'=2,'sub'=4] {'y','sub'}, dimensions={0} | all-to-all | bytes 32768 | tf_op jit(solution)/shard_map/all_to_all | solution.py:233
  139.5 17.3 %all_to_all.59.parts_ref = f32[24,1,128]{2,1,0:T(1,128)S(1)} all-to-all(f32[24,1,128]{2,1,0:T(1,128)S(1)} %broadcast_in_dim.35), channel_id=1, replica_groups=mesh['y'=8,'z'=12,'core'=2,'sub'=4] {'z','core'}, dimensions={0} | all-to-all | bytes 24576 | tf_op jit(solution)/shard_map/all_to_all | solution.py:233
  156.8 0.8 factor.1
  (17 shorter events, 0.1 us)
Async XLA Ops:
  0.6 21.8 %copy-start.1 = (f32[1,1,16,128]{3,2,1,0:T(8,128)S(1)}, f32[1,1,16,128]{3,2,1,0:T(8,128)}, u32[]{:S(2)}) copy-start(f32[1,1,16,128]{3,2,1,0:T(8,128)} %param.4) | copy-start | bytes 24580
  0.6 21.8 %copy-start.2 = (f32[8]{0:T(128)S(1)}, f32[8]{0:T(128)}, u32[]{:S(2)}) copy-start(f32[8]{0:T(128)} %param.7) | copy-start | bytes 100
  0.7 21.8 %copy-start.4 = (s32[1,1,16,7]{2,1,3,0:T(1,128)S(1)}, s32[1,1,16,7]{2,1,3,0:T(1,128)}, u32[]{:S(2)}) copy-start(s32[1,1,16,7]{2,1,3,0:T(1,128)} %param.6) | copy-start | bytes 1348
  0.7 21.8 %copy-start = (bf16[1,1,16,7,128,128]{5,4,3,2,1,0:T(8,128)(2,1)S(1)}, bf16[1,1,16,7,128,128]{5,4,3,2,1,0:T(8,128)(2,1)}, u32[]{:S(2)}) copy-start(bf16[1,1,16,7,128,128]{5,4,3,2,1,0:T(8,128)(2,1)} %param.5) | copy-start | bytes 11010052
  13.6 0.7 copy-start.3
